TPU v7x, 1024 devices: a whole 4x4x32 slice. The times are simulated.
1024 devices in a mesh: gx: 8 (over x, core), gy: 4 (over y), gz: 32 (over z).
Axes of the slice: x: 4, y: 4, z: 32, core: 2. Of those that a mesh axis runs over, the one named last changes fastest.
Arguments:
- state_velocity: float32 [3, 32, 16, 4096], P(None, 'gx', 'gy', 'gz'), may hold values from -3 to 3
- objective_gradient: float32 [3, 32, 16, 4096], P(None, 'gx', 'gy', 'gz'), may hold values from -15 to 15
- wall_flags: int32 [32, 16, 4096], P('gx', 'gy', 'gz'), may hold values 0 or 1
- design_levels: int32 [16, 8, 2048], P('gx', 'gy', 'gz'), may hold values from 0 to 8
Outputs:
- adjoint_velocity: float32 [3, 32, 16, 4096], P(None, 'gx', 'gy', 'gz')
- adjoint_pressure: float32 [16, 8, 2048], P('gx', 'gy', 'gz')
All inputs are finite; a program needn't handle non-finite values. No bound on the sum of `wall_flags` on one device may be relied on, other than what follows from the above.
Results may differ from a plain program's by a relative error of at most 0.0003.
Values sent between devices are 32-bit elements; how exact they have to be, the bound alone decides.
A program may use at most 64 MiB of HBM per device.

v0:
```python
import math

import jax
import jax.numpy as jnp
import numpy as np
from jax import lax
from jax.sharding import PartitionSpec as P

ITERS = 3
LEVELS = 9


viscosity = 1.0
brinkman_peak = 8.0
brinkman_shape = 0.1


def with_halo(cells, sides, width):
    for axis, dim in sides:
        count = lax.axis_size(axis)
        ends = count - 1
        head = lax.slice_in_dim(cells, 0, width, axis=dim)
        tail = lax.slice_in_dim(cells, cells.shape[dim] - width, cells.shape[dim], axis=dim)
        cells = jnp.concatenate(
            [
                lax.ppermute(tail, axis, [(i, (i + 1) % count) for i in range(ends)]),
                cells,
                lax.ppermute(head, axis, [((i + 1) % count, i) for i in range(ends)]),
            ],
            axis=dim,
        )
    return cells


def shape_values(abscissa):
    return (
        2.0 * (abscissa - 0.5) * (abscissa - 1.0),
        -4.0 * abscissa * (abscissa - 1.0),
        2.0 * abscissa * (abscissa - 0.5),
    )


def shape_slopes(abscissa):
    return (4.0 * abscissa - 3.0, 4.0 - 8.0 * abscissa, 4.0 * abscissa - 1.0)


def linear_values(abscissa):
    return (1.0 - abscissa, abscissa)


def flipped(matrix):
    return tuple((tuple((matrix[i][j] for i in range(len(matrix)))) for j in range(len(matrix[0]))))


def table_set():
    offset_value = math.sqrt(0.15)
    abscissae = (0.5 - offset_value, 0.5, 0.5 + offset_value)
    weight_list = np.array([5.0 / 18.0, 8.0 / 18.0, 5.0 / 18.0])
    value_matrix = tuple((shape_values(a) for a in abscissae))
    slope_matrix = tuple((shape_slopes(a) for a in abscissae))
    linear_matrix = tuple((linear_values(a) for a in abscissae))
    weight_grid = (
        weight_list[:, None, None] * weight_list[None, :, None] * weight_list[None, None, :]
    ).reshape(1, 3, 3, 3, 1, 1, 1)
    return (
        value_matrix,
        slope_matrix,
        linear_matrix,
        flipped(value_matrix),
        flipped(slope_matrix),
        flipped(linear_matrix),
        weight_grid,
    )


def pad_dim(values, dimension, before, after_count):
    widths = [(0, 0)] * values.ndim
    widths[dimension] = (before, after_count)
    return jnp.pad(values, widths)


def contract(element_vals, matrix, dimension):
    pieces = [
        lax.index_in_dim(element_vals, j, dimension, keepdims=False) for j in range(len(matrix[0]))
    ]
    outputs = []
    for coeffs in matrix:
        running = coeffs[0] * pieces[0]
        for j in range(1, len(coeffs)):
            running = running + coeffs[j] * pieces[j]
        outputs.append(running)
    return jnp.stack(outputs, axis=dimension)


def tensor(element_vals, along_x, along_y, along_z):
    return contract(contract(contract(element_vals, along_z, 3), along_y, 2), along_x, 1)


def split_dim(node_vals, linear):
    length = node_vals.shape[3]
    if linear:
        elements = length - 1
        parts = [
            lax.slice_in_dim(node_vals, 0, elements, axis=3),
            lax.slice_in_dim(node_vals, 1, length, axis=3),
        ]
    else:
        elements = (length - 1) // 2
        paired = node_vals.shape[:3] + (elements, 2) + node_vals.shape[4:]
        head_nodes = lax.slice_in_dim(node_vals, 0, 2 * elements, axis=3).reshape(paired)
        tail_nodes = lax.slice_in_dim(node_vals, 1, length, axis=3).reshape(paired)
        parts = [head_nodes[:, :, :, :, 0], head_nodes[:, :, :, :, 1], tail_nodes[:, :, :, :, 1]]
    return jnp.stack(parts, axis=1)


def gather_local(node_vals, linear):
    return split_dim(split_dim(split_dim(node_vals, linear), linear), linear)


def merge_dim(element_vals, linear):
    parts = [element_vals[:, j] for j in range(element_vals.shape[1])]
    if linear:
        return pad_dim(parts[0], 3, 0, 1) + pad_dim(parts[1], 3, 1, 0)
    elements = parts[0].shape[3]
    corner_nodes = pad_dim(parts[0], 3, 0, 1) + pad_dim(parts[2], 3, 1, 0)
    paired = jnp.stack([lax.slice_in_dim(corner_nodes, 0, elements, axis=3), parts[1]], axis=4)
    merged = paired.reshape(parts[1].shape[:3] + (2 * elements,) + parts[1].shape[4:])
    return jnp.concatenate(
        [merged, lax.slice_in_dim(corner_nodes, elements, elements + 1, axis=3)], axis=3
    )


def scatter_local(element_vals, linear):
    return merge_dim(merge_dim(merge_dim(element_vals, linear), linear), linear)


def brinkman_field(design_levels):
    density = design_levels.astype(jnp.float32) / (LEVELS - 1)
    coeff_field = brinkman_peak * brinkman_shape * (1.0 - density) / (brinkman_shape + density)
    return coeff_field.reshape((1, 1, 1, 1) + design_levels.shape)


def state_terms(state_nodes):
    value_matrix, slope_matrix = table_set()[0:2]
    element_vals = gather_local(state_nodes, False)
    quad_vals = tensor(element_vals, value_matrix, value_matrix, value_matrix)
    grads = (
        tensor(element_vals, slope_matrix, value_matrix, value_matrix),
        tensor(element_vals, value_matrix, slope_matrix, value_matrix),
        tensor(element_vals, value_matrix, value_matrix, slope_matrix),
    )
    return (quad_vals, grads)


def element_terms(velocity_local, pressure_local, state_quad, state_grads, brinkman):
    value_matrix, slope_matrix, linear_matrix, value_back, slope_back, linear_back, weight_grid = (
        table_set()
    )
    weights = jnp.asarray(weight_grid, dtype=jnp.float32)
    vel_quad = tensor(velocity_local, value_matrix, value_matrix, value_matrix)
    vel_grads = (
        tensor(velocity_local, slope_matrix, value_matrix, value_matrix),
        tensor(velocity_local, value_matrix, slope_matrix, value_matrix),
        tensor(velocity_local, value_matrix, value_matrix, slope_matrix),
    )
    pres_quad = tensor(pressure_local, linear_matrix, linear_matrix, linear_matrix)
    flux_terms = []
    for d in range(3):
        unit_column = jnp.asarray(np.eye(3)[:, d].reshape(3, 1, 1, 1, 1, 1, 1), dtype=jnp.float32)
        flux_terms.append(
            weights
            * (
                viscosity * vel_grads[d]
                + vel_quad * state_quad[d : d + 1]
                - pres_quad * unit_column
            )
        )
    transfer = jnp.stack([jnp.sum(state_grads[d] * vel_quad, axis=0) for d in range(3)])
    source = weights * (transfer + brinkman * vel_quad)
    divergence = -weights * (vel_grads[0][0:1] + vel_grads[1][1:2] + vel_grads[2][2:3])
    vel_out = (
        tensor(flux_terms[0], slope_back, value_back, value_back)
        + tensor(flux_terms[1], value_back, slope_back, value_back)
        + tensor(flux_terms[2], value_back, value_back, slope_back)
        + tensor(source, value_back, value_back, value_back)
    )
    pres_out = tensor(divergence, linear_back, linear_back, linear_back)
    return (vel_out, pres_out)


def least_squares(hessenberg, initial_norm):
    upper = [list(entries) for entries in hessenberg]
    target = [initial_norm] + [jnp.zeros((), jnp.float32) for j in range(ITERS)]
    for column in range(ITERS):
        diagonal = upper[column][column]
        below = upper[column + 1][column]
        radius = jnp.sqrt(diagonal * diagonal + below * below)
        cosine = diagonal / radius
        sine_part = below / radius
        for j in range(column, ITERS):
            upper_val = upper[column][j]
            lower_val = upper[column + 1][j]
            upper[column][j] = cosine * upper_val + sine_part * lower_val
            upper[column + 1][j] = cosine * lower_val - sine_part * upper_val
        upper_val = target[column]
        lower_val = target[column + 1]
        target[column] = cosine * upper_val + sine_part * lower_val
        target[column + 1] = cosine * lower_val - sine_part * upper_val
    coeffs = [None] * ITERS
    for column in reversed(range(ITERS)):
        running = target[column]
        for j in range(column + 1, ITERS):
            running = running - upper[column][j] * coeffs[j]
        coeffs[column] = running / upper[column][column]
    return coeffs


def fold_rims(halo_vals, dimension):
    length = halo_vals.shape[dimension]
    middle = lax.slice_in_dim(halo_vals, 1, length - 1, axis=dimension)
    lower_rim = lax.slice_in_dim(halo_vals, 0, 1, axis=dimension)
    upper_rim = lax.slice_in_dim(halo_vals, length - 1, length, axis=dimension)
    return (
        middle
        + pad_dim(lower_rim, dimension, 0, length - 3)
        + pad_dim(upper_rim, dimension, length - 3, 0)
    )


def assemble(partial_sums):
    extended = with_halo(partial_sums, (("gx", 1), ("gy", 2), ("gz", 3)), 1)
    return fold_rims(fold_rims(fold_rims(extended, 1), 2), 3)


def local_product(first_vec, second_vec):
    return jnp.sum(first_vec[:, :-1, :-1, :-1] * second_vec[:, :-1, :-1, :-1])


def global_products(stacked):
    return lax.psum(stacked, ("gx", "gy", "gz"))


def local(state_velocity, objective_gradient, wall_flags, design_levels):
    keep_owned = 1.0 - wall_flags.astype(jnp.float32)
    stacked = jnp.concatenate([state_velocity, objective_gradient, keep_owned[None]], axis=0)
    extended = assemble(jnp.pad(stacked, ((0, 0), (0, 1), (0, 1), (0, 1))))
    state_nodes = extended[0:3]
    keep_mask = extended[6:7]
    right_full = jnp.concatenate([extended[3:6], jnp.zeros_like(keep_mask)], axis=0)
    x_elements, y_elements, z_elements = design_levels.shape
    live_x = (jnp.arange(x_elements + 1) < x_elements) | (
        lax.axis_index("gx") < lax.axis_size("gx") - 1
    )
    live_y = (jnp.arange(y_elements + 1) < y_elements) | (
        lax.axis_index("gy") < lax.axis_size("gy") - 1
    )
    live_z = (jnp.arange(z_elements + 1) < z_elements) | (
        lax.axis_index("gz") < lax.axis_size("gz") - 1
    )
    keep_vertices = (live_x[:, None, None] & live_y[None, :, None] & live_z[None, None, :]).astype(
        jnp.float32
    )
    keep_pres_nodes = lax.pad(
        keep_vertices, jnp.zeros((), jnp.float32), ((0, 0, 1), (0, 0, 1), (0, 0, 1))
    )
    keep_full = jnp.concatenate(
        [jnp.broadcast_to(keep_mask, (3,) + keep_mask.shape[1:]), keep_pres_nodes[None]], axis=0
    )
    brinkman = brinkman_field(design_levels)
    state_quad, state_grads = state_terms(state_nodes)
    squared_start = lax.psum(local_product(right_full, right_full), ("gx", "gy", "gz"))
    initial_norm = jnp.sqrt(squared_start)
    krylov_basis = [right_full / initial_norm]
    hessenberg = [[jnp.zeros((), jnp.float32) for j in range(ITERS)] for i in range(ITERS + 1)]
    for k in range(ITERS):
        vector = krylov_basis[k]
        velocity = keep_full[:3] * vector[:3]
        pressure = vector[3:4, ::2, ::2, ::2]
        vel_out, pres_out = element_terms(
            gather_local(velocity, False),
            gather_local(pressure, True),
            state_quad,
            state_grads,
            brinkman,
        )
        vel_nodes = scatter_local(vel_out, False)
        pres_vert = scatter_local(pres_out, True)
        pres_nodes = lax.pad(
            pres_vert, jnp.zeros((), pres_vert.dtype), ((0, 0, 0), (0, 0, 1), (0, 0, 1), (0, 0, 1))
        )
        summed = assemble(jnp.concatenate([vel_nodes, pres_nodes], axis=0))
        carried = jnp.concatenate(
            [(1.0 - keep_full[:3]) * vector[:3], jnp.zeros_like(vector[3:4])], axis=0
        )
        image_vec = keep_full * summed + carried
        products = [local_product(image_vec, krylov_basis[i]) for i in range(k + 1)]
        products.append(local_product(image_vec, image_vec))
        totals = global_products(jnp.stack(products))
        projections = [totals[i] for i in range(k + 1)]
        squared = totals[k + 1]
        remainder = squared
        for i in range(k + 1):
            remainder = remainder - projections[i] * projections[i]
        next_norm = jnp.sqrt(remainder)
        for i in range(k + 1):
            hessenberg[i][k] = projections[i]
        hessenberg[k + 1][k] = next_norm
        if k + 1 < ITERS:
            new_vec = image_vec
            for i in range(k + 1):
                new_vec = new_vec - projections[i] * krylov_basis[i]
            krylov_basis.append(new_vec / next_norm)
    coeffs = least_squares(hessenberg, initial_norm)
    result = coeffs[0] * krylov_basis[0]
    for i in range(1, ITERS):
        result = result + coeffs[i] * krylov_basis[i]
    return (result[:3, :-1, :-1, :-1], result[3, :-1:2, :-1:2, :-1:2])


def solution(mesh):
    in_specs = (
        P(None, "gx", "gy", "gz"),
        P(None, "gx", "gy", "gz"),
        P("gx", "gy", "gz"),
        P("gx", "gy", "gz"),
    )
    out_specs = (P(None, "gx", "gy", "gz"), P("gx", "gy", "gz"))
    return jax.shard_map(local, mesh=mesh, in_specs=in_specs, out_specs=out_specs, check_vma=False)
```

profile of v0, /device:TPU:1, one launch (start us, length us, event | category | flops | bytes accessed | tf_op | source)
XLA Modules:
  0.0 823.1 jit_solution(15381198533031464289)
XLA Ops:
  0.6 0.7 subtract_bitcast_fusion
  1.3 0.8 select_maximum_fusion.2
  2.1 16.1 %collective-permute-start.1 = (f32[7,1,5,129]{3,2,1,0:T(8,128)S(1)}, f32[7,1,5,129]{3,2,1,0:T(8,128)S(1)}, u32[]{:S(2)}, u32[]{:S(2)}) collective-permute-start(f32[7,1,5,129]{3,2,1,0:T(8,128)S(1)} %slice.1941), channel_id=1, source_target_pairs={{128,0},{256,128},{384,256},{512,384},{640,512},{768,640},{896,768... | collective-permute-start | bytes 54188 | tf_op jit(solution)/shard_map/ppermute | solution.py:28
  18.2 1.9 collective-permute-start
  20.2 1.2 collective-permute-done
  21.5 1.3 collective-permute-start.3
  22.8 4.0 collective-permute-start.2
  26.8 1.1 collective-permute-done.2
  28.1 1.3 collective-permute-start.5
  29.4 4.0 collective-permute-start.4
  34.0 1.2 collective-permute-done.5
  35.2 0.8 collective-permute-done.4
  38.3 161.7 %psum.28 = f32[]{:T(128)} all-reduce(f32[]{:T(128)} %fusion.100), channel_id=1, replica_groups=mesh['gx'=8,'gy'=4,'gz'=32] {'gx','gy','gz'}, use_global_device_ids=true, to_apply=%region_1.2 | all-reduce | flops 1 | bytes 8 | tf_op jit(solution)/shard_map/psum | solution.py:271
  203.3 1.0 fusion.161
  205.5 0.9 multiply_add_fusion.201
  208.5 0.7 copy.661
  209.5 1.0 fusion.160
  222.4 1.3 pad.245.clone
  223.8 1.2 copy.708
  225.4 2.6 collective-permute-start.7
  228.0 3.0 collective-permute-start.6
  231.1 0.9 collective-permute-done.6
  232.0 1.3 collective-permute-start.9
  233.3 4.0 collective-permute-start.8
  238.3 1.3 collective-permute-start.11
  239.6 4.3 collective-permute-start.10
  243.9 0.8 collective-permute-done.11
  244.7 0.9 collective-permute-done.10
  246.3 0.9 copy-done
  247.9 1.4 pad_maximum_fusion.141
  249.3 158.1 %psum.29 = f32[2]{0:T(128)S(1)} all-reduce(f32[2]{0:T(128)S(1)} %pad_maximum_fusion.141), channel_id=1, replica_groups=mesh['gx'=8,'gy'=4,'gz'=32] {'gx','gy','gz'}, use_global_device_ids=true, to_apply=%region_7.8 | all-reduce | flops 2 | bytes 16 | tf_op jit(solution)/shard_map/psum | solution.py:240
  413.7 0.8 fusion.159
  423.4 1.3 pad.264.clone
  424.8 1.2 copy.762
  426.5 2.6 collective-permute-start.13
  429.1 3.0 collective-permute-start.12
  432.1 0.9 collective-permute-done.12
  433.0 1.3 collective-permute-start.15
  434.3 4.0 collective-permute-start.14
  438.3 1.0 collective-permute-done.14
  439.4 1.3 collective-permute-start.17
  440.7 4.3 collective-permute-start.16
  445.0 0.8 collective-permute-done.17
  445.7 0.9 collective-permute-done.16
  447.3 0.8 copy-done.2
  448.9 1.9 pad_maximum_fusion.142
  450.8 157.4 %psum.30 = f32[3]{0:T(128)S(1)} all-reduce(f32[3]{0:T(128)S(1)} %pad_maximum_fusion.142), channel_id=1, replica_groups=mesh['gx'=8,'gy'=4,'gz'=32] {'gx','gy','gz'}, use_global_device_ids=true, to_apply=%region_14.15 | all-reduce | flops 3 | bytes 24 | tf_op jit(solution)/shard_map/psum | solution.py:240
  611.8 1.3 subtract_divide_fusion
  616.0 0.8 fusion.158
  625.8 1.3 pad.283.clone
  627.2 1.2 copy.797
  628.8 2.6 collective-permute-start.19
  631.4 3.0 collective-permute-start.18
  634.4 0.9 collective-permute-done.18
  635.3 1.3 collective-permute-start.21
  636.6 4.0 collective-permute-start.20
  643.4 1.3 collective-permute-start.23
  644.7 4.3 collective-permute-start.22
  650.4 1.0 collective-permute-done.22
  652.1 0.8 copy-done.1
  652.9 0.7 multiply_reduce_fusion.11
  653.6 2.5 pad_maximum_fusion.143
  656.2 156.3 %psum.31 = f32[4]{0:T(128)S(1)} all-reduce(f32[4]{0:T(128)S(1)} %pad_maximum_fusion.143), channel_id=1, replica_groups=mesh['gx'=8,'gy'=4,'gz'=32] {'gx','gy','gz'}, use_global_device_ids=true, to_apply=%region_22.23 | all-reduce | flops 4 | bytes 32 | tf_op jit(solution)/shard_map/psum | solution.py:240
  822.1 0.9 slice.1940
  (447 shorter events, 52.5 us)
Async XLA Ops:
  2.1 18.0 %copy-start.17 = (s32[2,2,64]{2,1,0:T(2,128)S(1)}, s32[2,2,64]{2,1,0:T(2,128)}, u32[]{:S(2)}) copy-start(s32[2,2,64]{2,1,0:T(2,128)} %param.19) | copy-start | bytes 3076
  2.1 18.1 %collective-permute-start.1 = (f32[7,1,5,129]{3,2,1,0:T(8,128)S(1)}, f32[7,1,5,129]{3,2,1,0:T(8,128)S(1)}, u32[]{:S(2)}, u32[]{:S(2)}) collective-permute-start(f32[7,1,5,129]{3,2,1,0:T(8,128)S(1)} %slice.1941), channel_id=1, source_target_pairs={{128,0},{256,128},{384,256},{512,384},{640,512},{768,640},{896,768... | collective-permute-start | bytes 54188 | tf_op jit(solution)/shard_map/ppermute | solution.py:28
  18.2 3.2 collective-permute-start
  21.5 5.3 collective-permute-start.3
  22.8 5.2 collective-permute-start.2
  28.1 7.1 collective-permute-start.5
  29.4 6.6 collective-permute-start.4
  34.0 2.5 copy-start.8
  36.8 0.7 copy-start.9
  212.9 0.8 copy-start.5
  212.9 0.8 copy-start.6
  213.0 0.8 copy-start.4
  214.9 0.7 copy-start.3
  214.9 0.7 copy-start.11
  214.9 0.7 copy-start.14
  215.6 0.7 copy-start.7
  217.8 0.7 copy-start.10
  225.4 5.6 collective-permute-start.7
  228.0 3.9 collective-permute-start.6
  231.9 5.3 copy-start.18
  232.0 5.8 collective-permute-start.9
  233.3 5.0 collective-permute-start.8
  238.3 6.4 collective-permute-start.11
  239.6 5.9 collective-permute-start.10
  246.3 0.9 copy-start
  418.1 0.7 copy-start.12
  418.2 0.7 copy-start.15
  426.5 5.6 collective-permute-start.13
  429.1 3.9 collective-permute-start.12
  433.0 5.3 collective-permute-start.15
  434.3 5.0 collective-permute-start.14
  439.4 6.4 collective-permute-start.17
  440.7 5.9 collective-permute-start.16
  447.2 0.9 copy-start.2
  620.5 0.7 copy-start.13
  620.5 0.7 copy-start.16
  628.8 5.6 collective-permute-start.19
  631.4 3.9 collective-permute-start.18
  635.3 7.9 collective-permute-start.21
  636.6 6.6 collective-permute-start.20
  643.4 6.9 collective-permute-start.23
  644.7 6.6 collective-permute-start.22
  652.0 0.9 copy-start.1
where the time goes:
time: 831 us; the launch traced here: 823 us
  blocking collectives  634 us (76%)
  starting transfers between devices  77.8 us (9%)
  other arithmetic  41.2 us (5%)
  local copies, waits for them, and re-layouts  36.1 us (4%)
  between operations  21.8 us (3%)
  waiting for transfers between devices  12.6 us (2%)
    psum x3, blocking collectives, global_products(): return lax.psum(stacked, ('gx', 'gy', 'gz'))  472 us
    psum x1, blocking collectives, local(): lax.psum(local_product(right_full, right_full), ('gx', 'gy', 'gz'))  162 us
    ppermute x12, starting transfers between devices, with_halo(): lax.ppermute(tail, axis, [(i, (i + 1) % count) for i in range(ends)])  43.7 us
    ppermute x12, starting transfers between devices, with_halo(): lax.ppermute(head, axis, [((i + 1) % count, i) for i in range(ends)])  34.1 us
  transfers between devices with their start and end apart: 24, of which 14 were waited for; matrix products, arithmetic and copies ran while one was open for 0% of the time, Pallas kernels for 0%

commit v1 on v0

v1 whole, which is shorter than its diff:
```python
import functools
import itertools
import math

import jax
import jax.numpy as jnp
from jax import lax
from jax.experimental import pallas as pl
from jax.experimental.pallas import tpu as pltpu
from jax.sharding import PartitionSpec as P

MESH = pl.DeviceIdType.MESH
F32 = jnp.float32
HIGHEST = lax.Precision.HIGHEST

LEVELS = 9
PEAK = 8.0
SHAPE = 0.1

OFFSET = math.sqrt(0.15)
RATIO = 5.0 / 8.0
SCALE = (8.0 / 18.0) ** 3

NEAR = [o for o in itertools.product((-1, 0, 1), repeat=3) if o != (0, 0, 0)]
PLANE = [o for o in NEAR if o[2] == 0]

SOURCE = {-1: (2, 4), 0: (0, 4), 1: (0, 3)}
TARGET = {-1: (0, 2), 0: (2, 6), 1: (6, 9)}


def forward_both(a, b, c):
    d = c - a
    w = (b + b) - (a + c)
    s = (4.0 * OFFSET) * w
    m = b - 0.3 * w
    e = OFFSET * d
    return (m - e, b, m + e), (d + s, d, d - s)


def forward_value(a, b, c):
    d = c - a
    w = (b + b) - (a + c)
    m = b - 0.3 * w
    e = OFFSET * d
    return (m - e, b, m + e)


def back_value(f):
    s = f[0] + f[2]
    a = (0.3 * RATIO) * s
    b = (OFFSET * RATIO) * (f[2] - f[0])
    return (a - b, f[1] + (0.4 * RATIO) * s, a + b)


def back_both(f, g):
    s = f[0] + f[2]
    b = (OFFSET * RATIO) * (f[2] - f[0]) + (RATIO * (g[0] + g[2]) + g[1])
    w = (4.0 * OFFSET * RATIO) * (g[0] - g[2])
    a = (0.3 * RATIO) * s - w
    return (a - b, f[1] + (0.4 * RATIO) * s + (w + w), a + b)


def forward_linear(a, b):
    m = 0.5 * (a + b)
    d = OFFSET * (b - a)
    return (m - d, m, m + d)


def back_linear(f):
    m = (0.5 * RATIO) * (f[0] + f[2]) + 0.5 * f[1]
    d = (OFFSET * RATIO) * (f[2] - f[0])
    return (m - d, m + d)


def next_lane(v):
    return pltpu.roll(v, 127, 1)


def last_lane(v):
    return pltpu.roll(v, 1, 1)


def next_row(v):
    return pltpu.roll(v, 7, 0)


def last_row(v):
    return pltpu.roll(v, 1, 0)


def half_turn(v):
    return pltpu.roll(v, 4, 0)


def spread(elements, chunk, fields):
    def one(ci, carry):
        along = []
        for j in range(3):
            even = elements[chunk, ci, j, 0]
            along.append(forward_both(even, elements[chunk, ci, j, 1], next_lane(even)))
        for q in range(3):
            value, slope = forward_both(*[along[j][0][q] for j in range(3)])
            zslope = forward_value(*[along[j][1][q] for j in range(3)])
            for p in range(3):
                fields[ci, 0, p * 3 + q] = value[p]
                fields[ci, 1, p * 3 + q] = slope[p]
                fields[ci, 2, p * 3 + q] = zslope[p]
        return carry

    lax.fori_loop(0, 9, one, 0)


def at_points(fields, line, c):
    value, xslope = forward_both(*[fields[c * 3 + i, 0, line] for i in range(3)])
    yslope = forward_value(*[fields[c * 3 + i, 1, line] for i in range(3)])
    zslope = forward_value(*[fields[c * 3 + i, 2, line] for i in range(3)])
    return value, xslope, yslope, zslope


def apply_operator(above_floor, elements, pressures, chunk, state, slopes, fields, qpoints, ppoints, out, pout):
    spread(elements, chunk, fields)
    if pressures is not None:
        corner = {}
        for i in range(2):
            for j in range(2):
                low = pressures[chunk, i * 2 + j]
                corner[i, j] = forward_linear(low, next_lane(low))
        for q in range(3):
            sides = [forward_linear(corner[i, 0][q], corner[i, 1][q]) for i in range(2)]
            for p in range(3):
                points = forward_linear(sides[0][p], sides[1][p])
                for r in range(3):
                    qpoints[p * 3 + q, r] = points[r]

    def one(line, carry):
        value, slope = [], []
        for c in range(3):
            v, gx, gy, gz = at_points(fields, line, c)
            value.append(v)
            slope.append((gx, gy, gz))
        force = [[None] * 3 for _ in range(3)]
        flux = [[[None] * 3 for _ in range(3)] for _ in range(3)]
        for r in range(3):
            ppoints[line, r] = slope[0][0][r] + slope[1][1][r] + slope[2][2][r]
            wind = [state[chunk, line, r, b] for b in range(3)]
            pressure = qpoints[line, r] if pressures is not None else None
            for a in range(3):
                for b in range(3):
                    g = slope[a][b][r] + value[a][r] * wind[b]
                    if a == b and pressures is not None:
                        g = g - pressure
                    flux[a][b][r] = g
                total = slopes[chunk, line, r, a * 3] * value[0][r]
                for c in range(1, 3):
                    total = total + slopes[chunk, line, r, a * 3 + c] * value[c][r]
                force[a][r] = total
        for c in range(3):
            first = back_both(force[c], flux[c][0])
            second = back_value(flux[c][1])
            third = back_value(flux[c][2])
            for i in range(3):
                fields[c * 3 + i, 0, line] = first[i]
                fields[c * 3 + i, 1, line] = second[i]
                fields[c * 3 + i, 2, line] = third[i]
        return carry

    lax.fori_loop(0, 9, one, 0)

    def gather(ci, carry):
        value, zslope = [], []
        for q in range(3):
            value.append(
                back_both(
                    [fields[ci, 0, p * 3 + q] for p in range(3)],
                    [fields[ci, 1, p * 3 + q] for p in range(3)],
                )
            )
            zslope.append(back_value([fields[ci, 2, p * 3 + q] for p in range(3)]))
        for j in range(3):
            nodes = back_both([value[q][j] for q in range(3)], [zslope[q][j] for q in range(3)])
            out[chunk, ci, j, 0] = nodes[0] + last_lane(jnp.where(above_floor, nodes[2], 0.0))
            out[chunk, ci, j, 1] = nodes[1]
        return carry

    lax.fori_loop(0, 9, gather, 0)
    rows = {}
    for q in range(3):
        sides = []
        for p in range(3):
            sides.append(back_linear([ppoints[p * 3 + q, r] for r in range(3)]))
        for i in range(2):
            rows[i, q] = back_linear([sides[p][i] for p in range(3)])
    for i in range(2):
        for j in range(2):
            low, high = back_linear([rows[i, q][j] for q in range(3)])
            pout[chunk, i * 2 + j] = low + last_lane(jnp.where(above_floor, high, 0.0))


def pick(row, k):
    lane = lax.broadcasted_iota(jnp.int32, (1, 128), 1)
    return jnp.sum(jnp.where(lane == k, row, 0.0), axis=1, keepdims=True)


def solve(row):
    entries = {}
    at = 0
    for i in range(4):
        for j in range(i, 4):
            entries[i, j] = pick(row, at) + pick(row, 10)
            at += 1
    m = [[entries[min(i, j), max(i, j)] for j in range(1, 4)] + [entries[0, i]] for i in range(1, 4)]
    for k in range(2):
        inverse = 1.0 / m[k][k]
        for i in range(k + 1, 3):
            factor = m[i][k] * inverse
            for j in range(k + 1, 4):
                m[i][j] = m[i][j] - factor * m[k][j]
    t = [None] * 3
    for k in (2, 1, 0):
        total = m[k][3]
        for j in range(k + 1, 3):
            total = total - m[k][j] * t[j]
        t[k] = total / m[k][k]
    return t


def kernel(sizes, state_in, grad_in, wall_in, level_in, vel_out, pres_out,
           raw, nodes, ends, reach, even, odd, stiff, u0, us, u1, u2, u3, p1, p2, p3, keep_e, friction,
           wind, slopes, fields, qpoints, ppoints, out, pout, block, side, natural, plane_sum, line_sum,
           near_send, near_recv, part_send, part_recv, plane_send, plane_recv, line_send, line_recv):
    gx, gy, gz = lax.axis_index("gx"), lax.axis_index("gy"), lax.axis_index("gz")

    def device(o):
        return tuple(lax.rem(a + d + n, n) for a, d, n in zip((gx, gy, gz), o, sizes))

    others = [(a, b, 0) for a in range(sizes[0]) for b in range(sizes[1]) if (a, b) != (0, 0)]
    along = [(0, 0, d) for d in range(1, sizes[2])]
    partners = {tuple(d % n for d, n in zip(o, sizes)) for o in NEAR + others + along}
    partners = sorted(partners - {(0, 0, 0)})

    side[...] = jnp.zeros_like(side)
    plane_sum[...] = jnp.zeros_like(plane_sum)
    line_sum[...] = jnp.zeros_like(line_sum)

    barrier = pltpu.get_barrier_semaphore()
    for o in partners:
        pl.semaphore_signal(barrier, inc=1, device_id=device(o), device_id_type=MESH)

    lane = lax.broadcasted_iota(jnp.int32, (8, 128), 1)
    sub = lax.broadcasted_iota(jnp.int32, (8, 128), 0)

    for x in range(4):
        spot = pl.ds((x % 2) * 4, 4)
        mask = 1.0 - wall_in[x].astype(F32)
        for c in range(3):
            raw[c, x // 2, spot] = mask * grad_in[c, x]
            raw[3 + c, x // 2, spot] = state_in[c, x]
        raw[6, x // 2, spot] = mask
    rows = lax.broadcasted_iota(jnp.int32, (128, 128), 0)
    cols = lax.broadcasted_iota(jnp.int32, (128, 128), 1)
    split = (rows == jnp.where(cols < 64, 2 * cols, 2 * cols - 127)).astype(F32)
    join = (cols == jnp.where(rows < 64, 2 * rows, 2 * rows - 127)).astype(F32)
    parted = jnp.dot(raw[0:7].reshape(112, 128), split, precision=HIGHEST, preferred_element_type=F32)
    parted = parted.reshape(7, 2, 8, 128)
    twice = (rows[:64] == jnp.where(cols[:64] < 64, cols[:64], cols[:64] - 64)).astype(F32)
    density = level_in[...].astype(F32) / (LEVELS - 1)
    drag = PEAK * SHAPE * (1.0 - density) / (SHAPE + density)
    for h in range(2):
        wide = jnp.dot(drag[h], twice, precision=HIGHEST, preferred_element_type=F32)
        for y in range(4):
            raw[7, h, y : y + 1] = wide[y // 2 : y // 2 + 1]
            raw[7, h, y + 4 : y + 5] = wide[y // 2 : y // 2 + 1]
    for h in range(2):
        first = jnp.zeros((8, 128), F32)
        last = jnp.zeros((8, 128), F32)
        for f in range(8):
            v = raw[7, h] if f == 6 else parted[6 if f == 7 else f, h]
            for xl in range(2):
                nodes[f, 2 + 2 * h + xl, 2:6] = v[4 * xl : 4 * xl + 4]
            go = 8 * f
            lower = (lane >= go) & (lane < go + 4)
            upper = (lane >= go + 4) & (lane < go + 8)
            first = jnp.where(lower, pltpu.roll(v, go, 1), first)
            first = jnp.where(upper, pltpu.roll(v, (go + 4 - 64) % 128, 1), first)
            last = jnp.where(lower, pltpu.roll(v, (go - 60) % 128, 1), last)
            last = jnp.where(upper, pltpu.roll(v, (go + 4 - 124) % 128, 1), last)
        for xl in range(2):
            ends[0, 2 * h + xl, 0:4] = last[4 * xl : 4 * xl + 4]
            ends[1, 2 * h + xl, 0:4] = first[4 * xl : 4 * xl + 4]

    pl.semaphore_wait(barrier, len(partners))

    sent = []
    received = []
    for n, o in enumerate(NEAR):
        sx, sy = -o[0], -o[1]
        (xs, xe), (ys, ye) = SOURCE[sx], SOURCE[sy]
        (tx, te), (ty, tf) = TARGET[sx], TARGET[sy]
        if o[2] == 0:
            top = 8 if sx >= 0 and sy >= 0 else 7
            source = nodes.at[0:top, 2 + xs : 2 + xe, 2 + ys : 2 + ye]
            target = nodes.at[0:top, tx:te, ty:tf]
        else:
            which = 0 if o[2] == 1 else 1
            source = ends.at[which, xs:xe, ys:ye]
            target = reach.at[which, tx:te, ty:tf]
        copy = pltpu.make_async_remote_copy(
            src_ref=source, dst_ref=target, send_sem=near_send.at[n], recv_sem=near_recv.at[n],
            device_id=device(o), device_id_type=MESH)
        copy.start()
        sent.append(copy)
        received.append(copy)

    ey = sub % 4 - 1
    z = jnp.where(lane < 96, lane, lane - 128)
    zmin = jnp.where(gz > 0, -3, 0)
    zmax = jnp.where(gz < sizes[2] - 1, 65, 63)
    in_z = (z >= zmin) & (z <= zmax)
    ymin = jnp.where(gy > 0, -1, 0)
    ymax = jnp.where(gy < sizes[1] - 1, 2, 1)
    xmin = jnp.where(gx > 0, -1, 0)
    xmax = jnp.where(gx < sizes[0] - 1, 2, 1)
    ex = [jnp.where(sub < 4, 0, 1), jnp.where(sub < 4, 2, -1)]
    real = [in_z & (ey >= ymin) & (ey <= ymax) & (e >= xmin) & (e <= xmax) for e in ex]
    narrow = [r & (ey <= 1) & (e <= 1) for r, e in zip(real, ex)]
    own_y = (ey >= 0) & (ey <= 1)
    own_wide = in_z & own_y
    own = own_y & (lane < 64)
    zlim = jnp.where(gz < sizes[2] - 1, 64, 96)
    node_z = (lane < 64) | (lane >= zlim)
    above_floor = lane < jnp.where(gz > 0, 128, 96)
    ylim = jnp.where(gy < sizes[1] - 1, 99, 6)
    xlim = jnp.where(gx < sizes[0] - 1, 99, 6)
    node_yz = [node_z & (sub + 8 * h < ylim) for h in range(2)]

    for copy in received:
        copy.wait_recv()

    def widen(x, carry):
        inside = jnp.where(x < xlim, 1.0, 0.0).astype(F32)
        for h in range(2):
            rows8 = pl.ds(8 * h, 8)
            below = reach[0, x, rows8]
            above = reach[1, x, rows8]
            for f in range(8 if h == 0 else 6):
                v = nodes[f, x, rows8]
                go = 8 * f
                e = jnp.where(lane < 96, pltpu.roll(above, (64 - go) % 128, 1), pltpu.roll(below, (124 - go) % 128, 1))
                e = jnp.where(lane < 64, v, e)
                if f == 6:
                    stiff[0, x] = e
                    continue
                ok = node_yz[h]
                if f == 7:
                    ok = ok & (sub >= 2) & (sub < 7)
                even[f, x, rows8] = jnp.where(ok, e * inside, 0.0)
                o = jnp.where(lane < 96, pltpu.roll(above, (60 - go) % 128, 1), pltpu.roll(below, (120 - go) % 128, 1))
                o = jnp.where(lane < 64, pltpu.roll(v, 64, 1), o)
                odd[f, x, rows8] = jnp.where(ok, o * inside, 0.0)
        return carry

    lax.fori_loop(0, 9, widen, 0)

    def to_elements(source, f, x, j):
        return source[f, x, pl.ds(j, 4, stride=2), :]

    def collect(first, target, masks):
        def one(ci, carry):
            c, i = ci // 3, ci % 3
            for j in range(3):
                for k, source in enumerate((even, odd)):
                    for chunk, (low, high) in enumerate(((2, 4), (6, 0))):
                        v = jnp.concatenate(
                            [to_elements(source, first + c, low + i, j), to_elements(source, first + c, high + i, j)], axis=0)
                        if masks is not None:
                            v = jnp.where(masks[chunk], v, 0.0)
                        target[chunk, ci, j, k] = v
            return carry

        lax.fori_loop(0, 9, one, 0)

    collect(0, u0, real)
    collect(3, us, None)
    for i in range(3):
        for j in range(3):
            for k, source in enumerate((even, odd)):
                keep_e[i, j, k] = SCALE * jnp.concatenate(
                    [to_elements(source, 7, 2 + i, j), to_elements(source, 7, 4 + i, j)], axis=0)
    for chunk, (low, high) in enumerate(((2, 4), (6, 0))):
        friction[chunk] = jnp.concatenate([to_elements(stiff, 0, low, 0), to_elements(stiff, 0, high, 0)], axis=0)

    def prepare(chunk, carry):
        spread(us, chunk, fields)

        def one(line, inner):
            for c in range(3):
                v, gx_, gy_, gz_ = at_points(fields, line, c)
                for r in range(3):
                    wind[chunk, line, r, c] = v[r]
                    for b, g in enumerate((gx_, gy_, gz_)):
                        slopes[chunk, line, r, b * 3 + c] = g[r] + friction[chunk] if b == c else g[r]
            return inner

        lax.fori_loop(0, 9, one, 0)
        return carry

    lax.fori_loop(0, 2, prepare, 0)

    def first_step(chunk, carry):
        apply_operator(above_floor, u0, None, chunk, wind, slopes, fields, qpoints, ppoints, out, pout)
        return carry

    lax.fori_loop(0, 2, first_step, 0)

    low_half = sub < 4

    def owners(source, at, last):
        total = {}
        for chunk in range(2):
            for i in range(last + 1):
                v = [at(source, chunk, i, j) for j in range(last + 1)]
                total[chunk, i, 0] = v[0] + last_row(v[last])
                for j in range(1, last):
                    total[chunk, i, j] = v[j]
        return total

    def close(total, last):
        full = {}
        edge = {}
        for j in range(last):
            before = half_turn(total[1, last, j])
            mine = half_turn(total[0, last, j])
            full[0, j] = total[0, 0, j] + jnp.where(low_half, before, mine)
            edge[j] = total[1, 0, j] + mine
            for i in range(1, last):
                full[i, j] = total[0, i, j]
        return full, edge

    def complete(full, edge, last):
        for j in range(last):
            full[last, j] = jnp.where(low_half, half_turn(full[0, j]), half_turn(edge[j]))
        for i in range(last + 1):
            full[i, last] = next_row(full[i, 0])
        return full

    def finish_first(c, carry):
        for k in range(2):
            total = owners(out, lambda s, chunk, i, j: s[chunk, c * 3 + i, j, k], 2)
            full = complete(*close(total, 2), 2)
            for i in range(3):
                for j in range(3):
                    u1[0, c * 3 + i, j, k] = jnp.where(own_wide, full[i, j] * keep_e[i, j, k], 0.0)
        return carry

    lax.fori_loop(0, 3, finish_first, 0)

    def vertex_mask(i, j):
        ok = own_wide & ((lane < 64) | (lane >= zlim))
        ylast = jnp.where(gy < sizes[1] - 1, 99, 2)
        xlast = jnp.where(gx < sizes[0] - 1, 99, 2)
        return ok & (ey + j < ylast) & (ex[0] + i < xlast)

    full = complete(*close(owners(pout, lambda s, chunk, i, j: s[chunk, i * 2 + j], 1), 1), 1)
    for i in range(2):
        for j in range(2):
            p1[0, i * 2 + j] = jnp.where(vertex_mask(i, j), -SCALE * full[i, j], 0.0)

    apply_operator(above_floor, u1, p1, 0, wind, slopes, fields, qpoints, ppoints, out, pout)

    def store_rows(plane, x, parity, v, step):
        block[plane, x, pl.ds(parity, 4, stride=step), :] = v

    for n in range(7):
        last = 2 if n < 6 else 1
        c, k = n // 2, n % 2

        def at(i, j):
            return out[0, c * 3 + i, j, k] if n < 6 else pout[0, i * 2 + j]

        for j in range(last):
            v = [at(i, 0) + last_row(at(i, last)) if j == 0 else at(i, j) for i in range(last + 1)]
            if n == 6:
                v = [-SCALE * w for w in v]
            step = 2 // last
            turned = [half_turn(w) for w in v]
            for i in range(last):
                store_rows(n, step * i, j, v[i][0:4], 2)
            store_rows(n, 2, j, (v[last] + turned[0])[0:4], 2)
            for i in range(1, last):
                store_rows(n, 2 + i, j, turned[i][0:4], 2)
            store_rows(n, 4, j, turned[last][0:4], 2)
    vertex_yz = jnp.where(node_yz[0], 1.0, 0.0)
    for x in range(5):
        inside = jnp.where(x + 2 < xlim, 1.0, 0.0).astype(F32)
        for k, source in enumerate((even, odd)):
            mask = SCALE * source[7, x + 2, 0:8]
            for c in range(3):
                block[2 * c + k, x] = block[2 * c + k, x] * mask
        if x % 2 == 0:
            odd_rows = sub % 2 == 1
            block[6, x] = jnp.where(odd_rows, 0.0, block[6, x] * (vertex_yz * inside))
        else:
            block[6, x] = jnp.zeros((8, 128), F32)

    received = []
    for n, o in enumerate(PLANE):
        sx, sy = -o[0], -o[1]
        xs, xe = {-1: (2, 5), 0: (0, 5), 1: (0, 1)}[sx]
        ys, ty, count = {-1: (4, 0, 3), 0: (0, 0, 8), 1: (2, 6, 1)}[sy]
        copy = pltpu.make_async_remote_copy(
            src_ref=block.at[:, xs:xe, ys : ys + count], dst_ref=side.at[n, :, 0 : xe - xs, ty : ty + count],
            send_sem=part_send.at[n], recv_sem=part_recv.at[n], device_id=device(o), device_id_type=MESH)
        copy.start()
        sent.append(copy)
        received.append(copy)

    have = {0: 1.0}
    have_x = {-1: jnp.where(gx > 0, 1.0, 0.0).astype(F32), 1: jnp.where(gx < sizes[0] - 1, 1.0, 0.0).astype(F32)}
    have_y = {-1: jnp.where(gy > 0, 1.0, 0.0).astype(F32), 1: jnp.where(gy < sizes[1] - 1, 1.0, 0.0).astype(F32)}
    for copy in received:
        copy.wait_recv()

    def part(n, plane, x):
        sx, sy = -PLANE[n][0], -PLANE[n][1]
        v = side[n, plane, x]
        if sx:
            v = v * have_x[sx]
        if sy:
            v = v * have_y[sy]
        return v

    slot = {(-o[0], -o[1]): n for n, o in enumerate(PLANE)}

    def join_parts(plane, target, f):
        for x in range(7):
            total = block[plane, x - 2] if x >= 2 else None
            for sx in (-1, 0, 1):
                lo, hi = {-1: (0, 2), 0: (2, 6), 1: (6, 6)}[sx]
                if not lo <= x <= hi:
                    continue
                for sy in (-1, 0, 1):
                    if (sx, sy) != (0, 0):
                        v = part(slot[sx, sy], plane, x - lo)
                        total = v if total is None else total + v
            target[f, x, 0:8] = total

    def join_component(c, carry):
        join_parts(2 * c, even, c)
        join_parts(2 * c + 1, odd, c)
        return carry

    lax.fori_loop(0, 3, join_component, 0)
    join_parts(6, even, 3)
    collect(0, u2, narrow)
    for i in range(2):
        for j in range(2):
            for chunk, (low, high) in enumerate(((2, 4), (6, 0))):
                v = jnp.concatenate(
                    [to_elements(even, 3, low + 2 * i, 2 * j), to_elements(even, 3, high + 2 * i, 2 * j)], axis=0)
                p2[chunk, i * 2 + j] = jnp.where(narrow[chunk], v, 0.0)

    def last_step(chunk, carry):
        apply_operator(above_floor, u2, p2, chunk, wind, slopes, fields, qpoints, ppoints, out, pout)
        return carry

    lax.fori_loop(0, 2, last_step, 0)

    def finish_last(c, carry):
        for k in range(2):
            total = owners(out, lambda s, chunk, i, j: s[chunk, c * 3 + i, j, k], 2)
            full, _ = close(total, 2)
            for i in range(2):
                for j in range(2):
                    u3[0, c * 3 + i, j, k] = full[i, j] * keep_e[i, j, k]
        return carry

    lax.fori_loop(0, 3, finish_last, 0)
    full, _ = close(owners(pout, lambda s, chunk, i, j: s[chunk, i * 2 + j], 1), 1)
    p3[0, 0] = -SCALE * full[0, 0]

    pairs = [(i, j) for i in range(4) for j in range(i, 4)]

    def products(c, sums):
        sums = list(sums)
        for i in range(2):
            for j in range(2):
                for k in range(2):
                    v = [u[0, c * 3 + i, j, k] for u in (u0, u1, u2, u3)]
                    for n, (a, b) in enumerate(pairs):
                        sums[n] = sums[n] + v[a] * v[b]
        return tuple(sums)

    sums = list(lax.fori_loop(0, 3, products, tuple(jnp.zeros((8, 128), F32) for _ in pairs)))
    ps = [None, p1[0, 0], p2[0, 0], p3[0, 0]]
    for n, (a, b) in enumerate(pairs):
        if a:
            sums[n] = sums[n] + ps[a] * ps[b]
    fixed = jnp.zeros((4, 128), F32)
    for x in range(4):
        held = wall_in[x].astype(F32)
        for c in range(3):
            v = held * grad_in[c, x]
            fixed = fixed + v * v
    single = lane[0:1]
    row = jnp.zeros((1, 128), F32)
    for n in range(10):
        total = jnp.sum(jnp.sum(jnp.where(own, sums[n], 0.0), axis=0, keepdims=True), axis=1, keepdims=True)
        row = jnp.where(single == n, total, row)
    total = jnp.sum(jnp.sum(fixed, axis=0, keepdims=True), axis=1, keepdims=True)
    row = jnp.where(single == 10, total, row)

    def exchange(offsets, buffer, value, send_sems, recv_sems):
        buffer[0] = value
        copies = []
        for n, o in enumerate(offsets):
            copy = pltpu.make_async_remote_copy(
                src_ref=buffer.at[0], dst_ref=buffer.at[n + 1], send_sem=send_sems.at[n], recv_sem=recv_sems.at[n],
                device_id=device(o), device_id_type=MESH)
            copy.start()
            copies.append(copy)
        return copies

    def gathered(copies, buffer):
        for copy in copies:
            copy.wait_recv()
        total = buffer[0]
        for n in range(len(copies)):
            total = total + buffer[n + 1]
        return total

    copies = exchange(others, plane_sum, row, plane_send, plane_recv)
    sent += copies

    for n, u in enumerate((u1, u2)):
        for c in range(3):
            packed = []
            for i in range(2):
                for j in range(2):
                    packed.append(jnp.where(lane < 64, u[0, c * 3 + i, j, 0], pltpu.roll(u[0, c * 3 + i, j, 1], 64, 1)))
            flat = jnp.concatenate(packed, axis=0)
            flat = jnp.dot(flat, join, precision=HIGHEST, preferred_element_type=F32)
            for i in range(2):
                for j in range(2):
                    at8 = (i * 2 + j) * 8
                    for e in range(2):
                        natural[n, c, 2 * e + i, pl.ds(j, 2, stride=2), :] = flat[at8 + 4 * e + 1 : at8 + 4 * e + 3]

    row = gathered(copies, plane_sum)
    copies = exchange(along, line_sum, row, line_send, line_recv)
    sent += copies
    row = gathered(copies, line_sum)
    t = solve(row)
    for x in range(4):
        free = wall_in[x] == 0
        for c in range(3):
            b = grad_in[c, x]
            v = t[1] * natural[0, c, x, 0:4] + t[2] * natural[1, c, x, 0:4]
            vel_out[c, x] = jnp.where(free, t[0] * b, (t[0] + t[1] + t[2]) * b) + v
    v = t[1] * p1[0, 0] + t[2] * p2[0, 0]
    for e in range(2):
        pres_out[e] = v[4 * e + 1 : 4 * e + 3, 0:64]

    for copy in sent:
        copy.wait_send()


def local(sizes, state_velocity, objective_gradient, wall_flags, design_levels):
    vm = pltpu.VMEM
    plane, line = sizes[0] * sizes[1], sizes[2]
    tile = (8, 128)
    scratch = [
        vm((8, 2) + tile, F32),
        vm((8, 9, 16, 128), F32),
        vm((2, 4) + tile, F32),
        vm((2, 9, 16, 128), F32),
        vm((8, 9, 16, 128), F32),
        vm((8, 9, 16, 128), F32),
        vm((1, 9) + tile, F32),
        vm((2, 9, 3, 2) + tile, F32),
        vm((2, 9, 3, 2) + tile, F32),
        vm((1, 9, 3, 2) + tile, F32),
        vm((2, 9, 3, 2) + tile, F32),
        vm((1, 9, 3, 2) + tile, F32),
        vm((1, 4) + tile, F32),
        vm((2, 4) + tile, F32),
        vm((1, 1) + tile, F32),
        vm((3, 3, 2) + tile, F32),
        vm((2,) + tile, F32),
        vm((2, 9, 3, 3) + tile, F32),
        vm((2, 9, 3, 9) + tile, F32),
        vm((9, 3, 9) + tile, F32),
        vm((9, 3) + tile, F32),
        vm((9, 3) + tile, F32),
        vm((2, 9, 3, 2) + tile, F32),
        vm((2, 4) + tile, F32),
        vm((7, 5) + tile, F32),
        vm((8, 7, 5) + tile, F32),
        vm((2, 3, 4) + tile, F32),
        vm((plane, 1, 128), F32),
        vm((line, 1, 128), F32),
    ]
    for count in (26, 8, plane - 1, line - 1):
        scratch += [pltpu.SemaphoreType.DMA((count,))] * 2
    return pl.pallas_call(
        functools.partial(kernel, sizes),
        out_shape=(
            jax.ShapeDtypeStruct((3, 4, 4, 128), F32),
            jax.ShapeDtypeStruct((2, 2, 64), F32),
        ),
        in_specs=[pl.BlockSpec(memory_space=pltpu.VMEM)] * 4,
        out_specs=[pl.BlockSpec(memory_space=pltpu.VMEM)] * 2,
        scratch_shapes=scratch,
        compiler_params=pltpu.CompilerParams(
            collective_id=0, has_side_effects=True, vmem_limit_bytes=48 * 1024 * 1024
        ),
    )(state_velocity, objective_gradient, wall_flags, design_levels)


def solution(mesh):
    in_specs = (
        P(None, "gx", "gy", "gz"),
        P(None, "gx", "gy", "gz"),
        P("gx", "gy", "gz"),
        P("gx", "gy", "gz"),
    )
    out_specs = (P(None, "gx", "gy", "gz"), P("gx", "gy", "gz"))
    sizes = tuple(mesh.shape[a] for a in ("gx", "gy", "gz"))
    return jax.shard_map(
        functools.partial(local, sizes), mesh=mesh, in_specs=in_specs, out_specs=out_specs, check_vma=False
    )
```

time: 831 us -> 75.1 us (0.09)
  blocking collectives: 634 us -> 0 us
  starting transfers between devices: 77.8 us -> 0 us
  Pallas kernels: 0 us -> 70.1 us
  other arithmetic: 41.2 us -> 0 us
  local copies, waits for them, and re-layouts: 36.1 us -> 4.03 us
  between operations: 21.8 us -> 0.65 us
  waiting for transfers between devices: 12.6 us -> 0 us
    psum x4 -> x0, blocking collectives: 634 us -> none  [the longest x3 472 us: global_products(): return lax.psum(stacked, ('gx', 'gy', 'gz'))]
    ppermute x24 -> x0, starting transfers between devices: 77.8 us -> none  [the longest x12 43.7 us: with_halo(): lax.ppermute(tail, axis, [(i, (i + 1) % count) for i in range(ends)])]
    pallas_call x0 -> x1, Pallas kernels: none -> 70.1 us  [local(): pl.pallas_call(functools.partial(kernel, sizes), out_shape=(jax.ShapeDtyp...]
    slice x82 -> x0, local copies, waits for them, and re-layouts: 17.5 us -> none  [the longest x12 4.32 us: split_dim(): tail_nodes[:, :, :, :, 1]]
    another operation x98 -> x0, other arithmetic: 13.1 us -> none  [the longest x3 5.81 us: local(): totals = global_products(jnp.stack(products))]
    add x114 -> x0, other arithmetic: 13 us -> none  [the longest x85 10 us: contract(): running = running + coeffs[j] * pieces[j]]
    ppermute x24 -> x0, waiting for transfers between devices: 12.6 us -> none  [the longest x12 9.83 us: with_halo(): lax.ppermute(tail, axis, [(i, (i + 1) % count) for i in range(ends)])]
  transfers between devices with their start and end apart: 24 -> 0, of which waited for: 14 -> 0; matrix products, arithmetic and copies ran while one was open for 0% -> 0% of each run, Pallas kernels for 0% -> 0%
where the time goes in v1:
time: 75.1 us; the launch traced here: 74.8 us
  Pallas kernels  70.1 us (93%)
  local copies, waits for them, and re-layouts  4.03 us (5%)
    pallas_call x1, Pallas kernels, local(): pl.pallas_call(functools.partial(kernel, sizes), out_shape=(jax.ShapeDtyp...  70.1 us
    unnamed x10, local copies, waits for them, and re-layouts  4.03 us

profile of v1, /device:TPU:1, one launch (start us, length us, event | category | flops | bytes accessed | tf_op | source)
XLA Modules:
  0.0 74.8 jit_solution(2555206436663446949)
XLA Ops:
  0.6 0.0 copy-start
  0.6 0.7 copy-done
  1.4 0.0 copy-start.1
  1.4 0.7 copy-done.1
  2.1 0.0 copy-start.2
  2.1 0.7 copy-done.2
  2.8 0.0 copy-start.3
  2.8 0.7 copy-done.3
  3.5 70.1 %shard_map.59 = (f32[3,4,4,128]{3,2,1,0:T(4,128)S(1)}, f32[2,2,64]{2,1,0:T(2,128)S(1)}) custom-call(f32[3,4,4,128]{3,2,1,0:T(4,128)S(1)} %copy-done, f32[3,4,4,128]{3,2,1,0:T(4,128)S(1)} %copy-done.1, s32[4,4,128]{2,1,0:T(4,128)S(1)} %copy-done.2, s32[2,2,64]{2,1,0:T(2,128)S(1)} %copy-done.3), custom_call_target="tpu_custom_call" | custom-call | tf_op jit(solution)/shard_map/pallas_call | solution.py:704
  73.6 0.6 copy.8
  74.2 0.6 copy.9
Async XLA Ops:
  0.6 0.7 copy-start
  1.4 0.7 copy-start.1
  2.1 0.7 copy-start.2
  2.8 0.7 copy-start.3

commit v2 on v1

--- a/solution.py
+++ b/solution.py
@@ -18,6 +18,12 @@
 SHAPE = 0.1
 
 OFFSET = math.sqrt(0.15)
+GREETED = 4
+
+SPREAD = 3
+LINES = 9
+GATHER = 3
+
 RATIO = 5.0 / 8.0
 SCALE = (8.0 / 18.0) ** 3
 
@@ -73,11 +79,11 @@
 
 
 def next_lane(v):
-    return pltpu.roll(v, 127, 1)
+    return pltpu.roll(v, 127, v.ndim - 1)
 
 
 def last_lane(v):
-    return pltpu.roll(v, 1, 1)
+    return pltpu.roll(v, 1, v.ndim - 1)
 
 
 def next_row(v):
@@ -92,28 +98,40 @@
     return pltpu.roll(v, 4, 0)
 
 
+def blocks(count, size, body):
+    if size == count:
+        body(0)
+        return
+
+    def one(n, carry):
+        body(n * size)
+        return carry
+
+    lax.fori_loop(0, count // size, one, 0)
+
+
 def spread(elements, chunk, fields):
-    def one(ci, carry):
+    def one(c):
+        at = pl.ds(c, SPREAD)
         along = []
         for j in range(3):
-            even = elements[chunk, ci, j, 0]
-            along.append(forward_both(even, elements[chunk, ci, j, 1], next_lane(even)))
+            even = elements[chunk, at, :, j, 0]
+            along.append(forward_both(even, elements[chunk, at, :, j, 1], next_lane(even)))
         for q in range(3):
             value, slope = forward_both(*[along[j][0][q] for j in range(3)])
             zslope = forward_value(*[along[j][1][q] for j in range(3)])
             for p in range(3):
-                fields[ci, 0, p * 3 + q] = value[p]
-                fields[ci, 1, p * 3 + q] = slope[p]
-                fields[ci, 2, p * 3 + q] = zslope[p]
-        return carry
-
-    lax.fori_loop(0, 9, one, 0)
-
-
-def at_points(fields, line, c):
-    value, xslope = forward_both(*[fields[c * 3 + i, 0, line] for i in range(3)])
-    yslope = forward_value(*[fields[c * 3 + i, 1, line] for i in range(3)])
-    zslope = forward_value(*[fields[c * 3 + i, 2, line] for i in range(3)])
+                fields[at, :, 0, p * 3 + q] = value[p]
+                fields[at, :, 1, p * 3 + q] = slope[p]
+                fields[at, :, 2, p * 3 + q] = zslope[p]
+
+    blocks(3, SPREAD, one)
+
+
+def at_points(fields, lines, c):
+    value, xslope = forward_both(*[fields[c, i, 0, lines] for i in range(3)])
+    yslope = forward_value(*[fields[c, i, 1, lines] for i in range(3)])
+    zslope = forward_value(*[fields[c, i, 2, lines] for i in range(3)])
     return value, xslope, yslope, zslope
 
 
@@ -130,64 +148,64 @@
             for p in range(3):
                 points = forward_linear(sides[0][p], sides[1][p])
                 for r in range(3):
-                    qpoints[p * 3 + q, r] = points[r]
-
-    def one(line, carry):
+                    qpoints[r, p * 3 + q] = points[r]
+
+    def one(line):
+        lines = pl.ds(line, LINES)
         value, slope = [], []
         for c in range(3):
-            v, gx, gy, gz = at_points(fields, line, c)
+            v, gx, gy, gz = at_points(fields, lines, c)
             value.append(v)
             slope.append((gx, gy, gz))
         force = [[None] * 3 for _ in range(3)]
         flux = [[[None] * 3 for _ in range(3)] for _ in range(3)]
         for r in range(3):
-            ppoints[line, r] = slope[0][0][r] + slope[1][1][r] + slope[2][2][r]
-            wind = [state[chunk, line, r, b] for b in range(3)]
-            pressure = qpoints[line, r] if pressures is not None else None
+            ppoints[r, lines] = slope[0][0][r] + slope[1][1][r] + slope[2][2][r]
+            wind = [state[chunk, r, b, lines] for b in range(3)]
+            pressure = qpoints[r, lines] if pressures is not None else None
             for a in range(3):
                 for b in range(3):
                     g = slope[a][b][r] + value[a][r] * wind[b]
                     if a == b and pressures is not None:
                         g = g - pressure
                     flux[a][b][r] = g
-                total = slopes[chunk, line, r, a * 3] * value[0][r]
+                total = slopes[chunk, r, a * 3, lines] * value[0][r]
                 for c in range(1, 3):
-                    total = total + slopes[chunk, line, r, a * 3 + c] * value[c][r]
+                    total = total + slopes[chunk, r, a * 3 + c, lines] * value[c][r]
                 force[a][r] = total
         for c in range(3):
             first = back_both(force[c], flux[c][0])
             second = back_value(flux[c][1])
             third = back_value(flux[c][2])
             for i in range(3):
-                fields[c * 3 + i, 0, line] = first[i]
-                fields[c * 3 + i, 1, line] = second[i]
-                fields[c * 3 + i, 2, line] = third[i]
-        return carry
-
-    lax.fori_loop(0, 9, one, 0)
-
-    def gather(ci, carry):
+                fields[c, i, 0, lines] = first[i]
+                fields[c, i, 1, lines] = second[i]
+                fields[c, i, 2, lines] = third[i]
+
+    blocks(9, LINES, one)
+
+    def gather(c):
+        at = pl.ds(c, GATHER)
         value, zslope = [], []
         for q in range(3):
             value.append(
                 back_both(
-                    [fields[ci, 0, p * 3 + q] for p in range(3)],
-                    [fields[ci, 1, p * 3 + q] for p in range(3)],
+                    [fields[at, :, 0, p * 3 + q] for p in range(3)],
+                    [fields[at, :, 1, p * 3 + q] for p in range(3)],
                 )
             )
-            zslope.append(back_value([fields[ci, 2, p * 3 + q] for p in range(3)]))
+            zslope.append(back_value([fields[at, :, 2, p * 3 + q] for p in range(3)]))
         for j in range(3):
             nodes = back_both([value[q][j] for q in range(3)], [zslope[q][j] for q in range(3)])
-            out[chunk, ci, j, 0] = nodes[0] + last_lane(jnp.where(above_floor, nodes[2], 0.0))
-            out[chunk, ci, j, 1] = nodes[1]
-        return carry
-
-    lax.fori_loop(0, 9, gather, 0)
+            out[chunk, at, :, j, 0] = nodes[0] + last_lane(jnp.where(above_floor, nodes[2], 0.0))
+            out[chunk, at, :, j, 1] = nodes[1]
+
+    blocks(3, GATHER, gather)
     rows = {}
     for q in range(3):
         sides = []
         for p in range(3):
-            sides.append(back_linear([ppoints[p * 3 + q, r] for r in range(3)]))
+            sides.append(back_linear([ppoints[r, p * 3 + q] for r in range(3)]))
         for i in range(2):
             rows[i, q] = back_linear([sides[p][i] for p in range(3)])
     for i in range(2):
@@ -224,10 +242,18 @@
     return t
 
 
-def kernel(sizes, state_in, grad_in, wall_in, level_in, vel_out, pres_out,
-           raw, nodes, ends, reach, even, odd, stiff, u0, us, u1, u2, u3, p1, p2, p3, keep_e, friction,
+def kernel(sizes, state_far, grad_far, wall_far, level_far, vel_out, pres_out,
+           state_in, grad_in, wall_in, level_in, raw, nodes, ends, reach, even, odd, stiff, u0, us, u1, u2, u3, p1, p2, p3, keep_e, friction,
            wind, slopes, fields, qpoints, ppoints, out, pout, block, side, natural, plane_sum, line_sum,
-           near_send, near_recv, part_send, part_recv, plane_send, plane_recv, line_send, line_recv):
+           load, reached, near_send, near_recv, part_send, part_recv, plane_send, plane_recv, line_send, line_recv):
+    loads = [
+        pltpu.make_async_copy(far, near, load.at[n])
+        for n, (far, near) in enumerate(
+            ((grad_far, grad_in), (state_far, state_in), (wall_far, wall_in), (level_far, level_in)))
+    ]
+    for copy in loads:
+        copy.start()
+
     gx, gy, gz = lax.axis_index("gx"), lax.axis_index("gy"), lax.axis_index("gz")
 
     def device(o):
@@ -235,12 +261,11 @@
 
     others = [(a, b, 0) for a in range(sizes[0]) for b in range(sizes[1]) if (a, b) != (0, 0)]
     along = [(0, 0, d) for d in range(1, sizes[2])]
-    partners = {tuple(d % n for d, n in zip(o, sizes)) for o in NEAR + others + along}
+    close_by = [(0, 0, d) for d in range(-GREETED, GREETED + 1)]
+    partners = {tuple(d % n for d, n in zip(o, sizes)) for o in NEAR + others + close_by}
     partners = sorted(partners - {(0, 0, 0)})
 
     side[...] = jnp.zeros_like(side)
-    plane_sum[...] = jnp.zeros_like(plane_sum)
-    line_sum[...] = jnp.zeros_like(line_sum)
 
     barrier = pltpu.get_barrier_semaphore()
     for o in partners:
@@ -248,6 +273,9 @@
 
     lane = lax.broadcasted_iota(jnp.int32, (8, 128), 1)
     sub = lax.broadcasted_iota(jnp.int32, (8, 128), 0)
+
+    for copy in loads:
+        copy.wait()
 
     for x in range(4):
         spot = pl.ds((x % 2) * 4, 4)
@@ -290,6 +318,17 @@
 
     pl.semaphore_wait(barrier, len(partners))
 
+    def tell(n):
+        for d in (-1, 1):
+            pl.semaphore_signal(
+                reached.at[n], inc=1, device_id=device((0, 0, d * GREETED * 2**n)), device_id_type=MESH)
+
+    rounds = 0
+    while GREETED * 2**rounds < sizes[2] // 2:
+        rounds += 1
+    if rounds:
+        tell(0)
+
     sent = []
     received = []
     for n, o in enumerate(NEAR):
@@ -335,6 +374,9 @@
 
     for copy in received:
         copy.wait_recv()
+    for n in range(1, rounds):
+        pl.semaphore_wait(reached.at[n - 1], 2)
+        tell(n)
 
     def widen(x, carry):
         inside = jnp.where(x < xlim, 1.0, 0.0).astype(F32)
@@ -365,19 +407,16 @@
         return source[f, x, pl.ds(j, 4, stride=2), :]
 
     def collect(first, target, masks):
-        def one(ci, carry):
-            c, i = ci // 3, ci % 3
+        three = pl.ds(first, 3)
+        for i in range(3):
             for j in range(3):
                 for k, source in enumerate((even, odd)):
                     for chunk, (low, high) in enumerate(((2, 4), (6, 0))):
                         v = jnp.concatenate(
-                            [to_elements(source, first + c, low + i, j), to_elements(source, first + c, high + i, j)], axis=0)
+                            [to_elements(source, three, low + i, j), to_elements(source, three, high + i, j)], axis=1)
                         if masks is not None:
                             v = jnp.where(masks[chunk], v, 0.0)
-                        target[chunk, ci, j, k] = v
-            return carry
-
-        lax.fori_loop(0, 9, one, 0)
+                        target[chunk, :, i, j, k] = v
 
     collect(0, u0, real)
     collect(3, us, None)
@@ -392,16 +431,16 @@
     def prepare(chunk, carry):
         spread(us, chunk, fields)
 
-        def one(line, inner):
+        def one(line):
+            lines = pl.ds(line, LINES)
             for c in range(3):
-                v, gx_, gy_, gz_ = at_points(fields, line, c)
+                v, gx_, gy_, gz_ = at_points(fields, lines, c)
                 for r in range(3):
-                    wind[chunk, line, r, c] = v[r]
+                    wind[chunk, r, c, lines] = v[r]
                     for b, g in enumerate((gx_, gy_, gz_)):
-                        slopes[chunk, line, r, b * 3 + c] = g[r] + friction[chunk] if b == c else g[r]
-            return inner
-
-        lax.fori_loop(0, 9, one, 0)
+                        slopes[chunk, r, b * 3 + c, lines] = g[r] + friction[chunk] if b == c else g[r]
+
+        blocks(9, LINES, one)
         return carry
 
     lax.fori_loop(0, 2, prepare, 0)
@@ -445,11 +484,11 @@
 
     def finish_first(c, carry):
         for k in range(2):
-            total = owners(out, lambda s, chunk, i, j: s[chunk, c * 3 + i, j, k], 2)
+            total = owners(out, lambda s, chunk, i, j: s[chunk, c, i, j, k], 2)
             full = complete(*close(total, 2), 2)
             for i in range(3):
                 for j in range(3):
-                    u1[0, c * 3 + i, j, k] = jnp.where(own_wide, full[i, j] * keep_e[i, j, k], 0.0)
+                    u1[0, c, i, j, k] = jnp.where(own_wide, full[i, j] * keep_e[i, j, k], 0.0)
         return carry
 
     lax.fori_loop(0, 3, finish_first, 0)
@@ -475,7 +514,7 @@
         c, k = n // 2, n % 2
 
         def at(i, j):
-            return out[0, c * 3 + i, j, k] if n < 6 else pout[0, i * 2 + j]
+            return out[0, c, i, j, k] if n < 6 else pout[0, i * 2 + j]
 
         for j in range(last):
             v = [at(i, 0) + last_row(at(i, last)) if j == 0 else at(i, j) for i in range(last + 1)]
@@ -567,11 +606,11 @@
 
     def finish_last(c, carry):
         for k in range(2):
-            total = owners(out, lambda s, chunk, i, j: s[chunk, c * 3 + i, j, k], 2)
+            total = owners(out, lambda s, chunk, i, j: s[chunk, c, i, j, k], 2)
             full, _ = close(total, 2)
             for i in range(2):
                 for j in range(2):
-                    u3[0, c * 3 + i, j, k] = full[i, j] * keep_e[i, j, k]
+                    u3[0, c, i, j, k] = full[i, j] * keep_e[i, j, k]
         return carry
 
     lax.fori_loop(0, 3, finish_last, 0)
@@ -585,7 +624,7 @@
         for i in range(2):
             for j in range(2):
                 for k in range(2):
-                    v = [u[0, c * 3 + i, j, k] for u in (u0, u1, u2, u3)]
+                    v = [u[0, c, i, j, k] for u in (u0, u1, u2, u3)]
                     for n, (a, b) in enumerate(pairs):
                         sums[n] = sums[n] + v[a] * v[b]
         return tuple(sums)
@@ -636,7 +675,7 @@
             packed = []
             for i in range(2):
                 for j in range(2):
-                    packed.append(jnp.where(lane < 64, u[0, c * 3 + i, j, 0], pltpu.roll(u[0, c * 3 + i, j, 1], 64, 1)))
+                    packed.append(jnp.where(lane < 64, u[0, c, i, j, 0], pltpu.roll(u[0, c, i, j, 1], 64, 1)))
             flat = jnp.concatenate(packed, axis=0)
             flat = jnp.dot(flat, join, precision=HIGHEST, preferred_element_type=F32)
             for i in range(2):
@@ -646,6 +685,8 @@
                         natural[n, c, 2 * e + i, pl.ds(j, 2, stride=2), :] = flat[at8 + 4 * e + 1 : at8 + 4 * e + 3]
 
     row = gathered(copies, plane_sum)
+    if rounds:
+        pl.semaphore_wait(reached.at[rounds - 1], 2)
     copies = exchange(along, line_sum, row, line_send, line_recv)
     sent += copies
     row = gathered(copies, line_sum)
@@ -669,6 +710,10 @@
     plane, line = sizes[0] * sizes[1], sizes[2]
     tile = (8, 128)
     scratch = [
+        vm((3, 4, 4, 128), F32),
+        vm((3, 4, 4, 128), F32),
+        vm((4, 4, 128), jnp.int32),
+        vm((2, 2, 64), jnp.int32),
         vm((8, 2) + tile, F32),
         vm((8, 9, 16, 128), F32),
         vm((2, 4) + tile, F32),
@@ -676,22 +721,22 @@
         vm((8, 9, 16, 128), F32),
         vm((8, 9, 16, 128), F32),
         vm((1, 9) + tile, F32),
-        vm((2, 9, 3, 2) + tile, F32),
-        vm((2, 9, 3, 2) + tile, F32),
-        vm((1, 9, 3, 2) + tile, F32),
-        vm((2, 9, 3, 2) + tile, F32),
-        vm((1, 9, 3, 2) + tile, F32),
+        vm((2, 3, 3, 3, 2) + tile, F32),
+        vm((2, 3, 3, 3, 2) + tile, F32),
+        vm((1, 3, 3, 3, 2) + tile, F32),
+        vm((2, 3, 3, 3, 2) + tile, F32),
+        vm((1, 3, 3, 3, 2) + tile, F32),
         vm((1, 4) + tile, F32),
         vm((2, 4) + tile, F32),
         vm((1, 1) + tile, F32),
         vm((3, 3, 2) + tile, F32),
         vm((2,) + tile, F32),
-        vm((2, 9, 3, 3) + tile, F32),
-        vm((2, 9, 3, 9) + tile, F32),
-        vm((9, 3, 9) + tile, F32),
-        vm((9, 3) + tile, F32),
-        vm((9, 3) + tile, F32),
-        vm((2, 9, 3, 2) + tile, F32),
+        vm((2, 3, 3, 9) + tile, F32),
+        vm((2, 3, 9, 9) + tile, F32),
+        vm((3, 3, 3, 9) + tile, F32),
+        vm((3, 9) + tile, F32),
+        vm((3, 9) + tile, F32),
+        vm((2, 3, 3, 3, 2) + tile, F32),
         vm((2, 4) + tile, F32),
         vm((7, 5) + tile, F32),
         vm((8, 7, 5) + tile, F32),
@@ -699,6 +744,7 @@
         vm((plane, 1, 128), F32),
         vm((line, 1, 128), F32),
     ]
+    scratch += [pltpu.SemaphoreType.DMA((4,)), pltpu.SemaphoreType.REGULAR((4,))]
     for count in (26, 8, plane - 1, line - 1):
         scratch += [pltpu.SemaphoreType.DMA((count,))] * 2
     return pl.pallas_call(
@@ -707,11 +753,11 @@
             jax.ShapeDtypeStruct((3, 4, 4, 128), F32),
             jax.ShapeDtypeStruct((2, 2, 64), F32),
         ),
-        in_specs=[pl.BlockSpec(memory_space=pltpu.VMEM)] * 4,
+        in_specs=[pl.BlockSpec(memory_space=pl.ANY)] * 4,
         out_specs=[pl.BlockSpec(memory_space=pltpu.VMEM)] * 2,
         scratch_shapes=scratch,
         compiler_params=pltpu.CompilerParams(
-            collective_id=0, has_side_effects=True, vmem_limit_bytes=48 * 1024 * 1024
+            collective_id=0, has_side_effects=True, vmem_limit_bytes=56 * 1024 * 1024
         ),
     )(state_velocity, objective_gradient, wall_flags, design_levels)
 

time: 75.1 us -> 60.8 us (0.81)
  Pallas kernels: 70.1 us -> 58 us
  local copies, waits for them, and re-layouts: 4.03 us -> 1.93 us
    pallas_call x1, Pallas kernels: 70.1 us -> 58 us  [local(): pl.pallas_call(functools.partial(kernel, sizes), out_shape=(jax.ShapeDtyp...]
    unnamed x10 -> x4, local copies, waits for them, and re-layouts: 4.03 us -> 1.93 us
where the time goes in v2:
time: 60.8 us; the launch traced here: 60.5 us
  Pallas kernels  58 us (95%)
  local copies, waits for them, and re-layouts  1.93 us (3%)
  between operations  0.65 us (1%)
    pallas_call x1, Pallas kernels, local(): pl.pallas_call(functools.partial(kernel, sizes), out_shape=(jax.ShapeDtyp...  58 us
    unnamed x4, local copies, waits for them, and re-layouts  1.93 us

profile of v2, /device:TPU:1, one launch (start us, length us, event | category | flops | bytes accessed | tf_op | source)
XLA Modules:
  0.0 60.5 jit_solution(7284858542347739525)
XLA Ops:
  0.6 58.0 %shard_map.59 = (f32[3,4,4,128]{3,2,1,0:T(4,128)}, f32[2,2,64]{2,1,0:T(2,128)}) custom-call(f32[3,4,4,128]{3,2,1,0:T(4,128)} %state_far.1, f32[3,4,4,128]{3,2,1,0:T(4,128)} %grad_far.1, s32[4,4,128]{2,1,0:T(4,128)} %wall_far.1, s32[2,2,64]{2,1,0:T(2,128)} %level_far.1), custom_call_target="tpu_custom_call" | custom-call | tf_op jit(solution)/shard_map/pallas_call | solution.py:750
  58.6 0.0 copy-start
  58.6 1.3 %copy.8 = f32[3,4,4,128]{3,2,1,0:T(4,128)} copy(f32[3,4,4,128]{3,2,1,0:T(4,128)} %get-tuple-element.4) | data formatting | bytes 49152
  60.0 0.0 copy-done
  60.0 0.6 copy.9
Async XLA Ops:
  58.6 1.4 %copy-start = (f32[2,2,64]{2,1,0:T(2,128)S(1)}, f32[2,2,64]{2,1,0:T(2,128)}, u32[]{:S(2)}) copy-start(f32[2,2,64]{2,1,0:T(2,128)} %get-tuple-element.5) | copy-start | bytes 3076

commit v3 on v2

--- a/solution.py
+++ b/solution.py
@@ -18,8 +18,6 @@
 SHAPE = 0.1
 
 OFFSET = math.sqrt(0.15)
-GREETED = 4
-
 SPREAD = 3
 LINES = 9
 GATHER = 3
@@ -28,6 +26,7 @@
 SCALE = (8.0 / 18.0) ** 3
 
 NEAR = [o for o in itertools.product((-1, 0, 1), repeat=3) if o != (0, 0, 0)]
+NEAR.sort(key=lambda o: (o[2] == 0, -sum(map(abs, o))))
 PLANE = [o for o in NEAR if o[2] == 0]
 
 SOURCE = {-1: (2, 4), 0: (0, 4), 1: (0, 3)}
@@ -245,7 +244,7 @@
 def kernel(sizes, state_far, grad_far, wall_far, level_far, vel_out, pres_out,
            state_in, grad_in, wall_in, level_in, raw, nodes, ends, reach, even, odd, stiff, u0, us, u1, u2, u3, p1, p2, p3, keep_e, friction,
            wind, slopes, fields, qpoints, ppoints, out, pout, block, side, natural, plane_sum, line_sum,
-           load, reached, near_send, near_recv, part_send, part_recv, plane_send, plane_recv, line_send, line_recv):
+           load, reached, across, send, recv):
     loads = [
         pltpu.make_async_copy(far, near, load.at[n])
         for n, (far, near) in enumerate(
@@ -261,8 +260,7 @@
 
     others = [(a, b, 0) for a in range(sizes[0]) for b in range(sizes[1]) if (a, b) != (0, 0)]
     along = [(0, 0, d) for d in range(1, sizes[2])]
-    close_by = [(0, 0, d) for d in range(-GREETED, GREETED + 1)]
-    partners = {tuple(d % n for d, n in zip(o, sizes)) for o in NEAR + others + close_by}
+    partners = {tuple(d % n for d, n in zip(o, sizes)) for o in NEAR}
     partners = sorted(partners - {(0, 0, 0)})
 
     side[...] = jnp.zeros_like(side)
@@ -321,34 +319,42 @@
     def tell(n):
         for d in (-1, 1):
             pl.semaphore_signal(
-                reached.at[n], inc=1, device_id=device((0, 0, d * GREETED * 2**n)), device_id_type=MESH)
+                reached.at[n], inc=1, device_id=device((0, 0, d * 2**n)), device_id_type=MESH)
 
     rounds = 0
-    while GREETED * 2**rounds < sizes[2] // 2:
+    while 2**rounds < sizes[2] // 2:
         rounds += 1
     if rounds:
         tell(0)
 
-    sent = []
-    received = []
-    for n, o in enumerate(NEAR):
+    for o in NEAR:
         sx, sy = -o[0], -o[1]
         (xs, xe), (ys, ye) = SOURCE[sx], SOURCE[sy]
         (tx, te), (ty, tf) = TARGET[sx], TARGET[sy]
         if o[2] == 0:
-            top = 8 if sx >= 0 and sy >= 0 else 7
-            source = nodes.at[0:top, 2 + xs : 2 + xe, 2 + ys : 2 + ye]
-            target = nodes.at[0:top, tx:te, ty:tf]
+            source = nodes.at[:, 2 + xs : 2 + xe, 2 + ys : 2 + ye]
+            target = nodes.at[:, tx:te, ty:tf]
+            group = 0
         else:
+            group = 1
             which = 0 if o[2] == 1 else 1
             source = ends.at[which, xs:xe, ys:ye]
             target = reach.at[which, tx:te, ty:tf]
-        copy = pltpu.make_async_remote_copy(
-            src_ref=source, dst_ref=target, send_sem=near_send.at[n], recv_sem=near_recv.at[n],
-            device_id=device(o), device_id_type=MESH)
-        copy.start()
-        sent.append(copy)
-        received.append(copy)
+        pltpu.make_async_remote_copy(
+            src_ref=source, dst_ref=target, send_sem=send.at[group], recv_sem=recv.at[group],
+            device_id=device(o), device_id_type=MESH).start()
+
+    in_all = [
+        nodes.at[:, 0:5, 0:13],
+        reach.at[:, :, 0:9],
+        side.at[0:7, :, 0:1],
+        plane_sum.at[1 : len(others) + 1],
+        line_sum.at[1 : len(along) + 1],
+    ]
+
+    def arrived(group):
+        ref = in_all[group]
+        pltpu.make_async_copy(ref, ref, recv.at[group]).wait()
 
     ey = sub % 4 - 1
     z = jnp.where(lane < 96, lane, lane - 128)
@@ -372,11 +378,14 @@
     xlim = jnp.where(gx < sizes[0] - 1, 99, 6)
     node_yz = [node_z & (sub + 8 * h < ylim) for h in range(2)]
 
-    for copy in received:
-        copy.wait_recv()
-    for n in range(1, rounds):
-        pl.semaphore_wait(reached.at[n - 1], 2)
-        tell(n)
+    if rounds > 1:
+        pl.semaphore_wait(reached.at[0], 2)
+        tell(1)
+    arrived(0)
+    arrived(1)
+    if sizes[0] > 6:
+        for d in (-2, 2):
+            pl.semaphore_signal(across, inc=1, device_id=device((d, 0, 0)), device_id_type=MESH)
 
     def widen(x, carry):
         inside = jnp.where(x < xlim, 1.0, 0.0).astype(F32)
@@ -503,6 +512,10 @@
     for i in range(2):
         for j in range(2):
             p1[0, i * 2 + j] = jnp.where(vertex_mask(i, j), -SCALE * full[i, j], 0.0)
+
+    if rounds > 2:
+        pl.semaphore_wait(reached.at[1], 2)
+        tell(2)
 
     apply_operator(above_floor, u1, p1, 0, wind, slopes, fields, qpoints, ppoints, out, pout)
 
@@ -541,23 +554,21 @@
         else:
             block[6, x] = jnp.zeros((8, 128), F32)
 
-    received = []
     for n, o in enumerate(PLANE):
         sx, sy = -o[0], -o[1]
         xs, xe = {-1: (2, 5), 0: (0, 5), 1: (0, 1)}[sx]
-        ys, ty, count = {-1: (4, 0, 3), 0: (0, 0, 8), 1: (2, 6, 1)}[sy]
-        copy = pltpu.make_async_remote_copy(
+        ys, ty, count = {-1: (4, 0, 3), 0: (2, 2, 5), 1: (2, 6, 1)}[sy]
+        pltpu.make_async_remote_copy(
             src_ref=block.at[:, xs:xe, ys : ys + count], dst_ref=side.at[n, :, 0 : xe - xs, ty : ty + count],
-            send_sem=part_send.at[n], recv_sem=part_recv.at[n], device_id=device(o), device_id_type=MESH)
-        copy.start()
-        sent.append(copy)
-        received.append(copy)
+            send_sem=send.at[2], recv_sem=recv.at[2], device_id=device(o), device_id_type=MESH).start()
 
     have = {0: 1.0}
     have_x = {-1: jnp.where(gx > 0, 1.0, 0.0).astype(F32), 1: jnp.where(gx < sizes[0] - 1, 1.0, 0.0).astype(F32)}
     have_y = {-1: jnp.where(gy > 0, 1.0, 0.0).astype(F32), 1: jnp.where(gy < sizes[1] - 1, 1.0, 0.0).astype(F32)}
-    for copy in received:
-        copy.wait_recv()
+    arrived(2)
+    if rounds > 3:
+        pl.semaphore_wait(reached.at[2], 2)
+        tell(3)
 
     def part(n, plane, x):
         sx, sy = -PLANE[n][0], -PLANE[n][1]
@@ -648,27 +659,20 @@
     total = jnp.sum(jnp.sum(fixed, axis=0, keepdims=True), axis=1, keepdims=True)
     row = jnp.where(single == 10, total, row)
 
-    def exchange(offsets, buffer, value, send_sems, recv_sems):
+    def exchange(group, offsets, buffer, value):
         buffer[0] = value
-        copies = []
         for n, o in enumerate(offsets):
-            copy = pltpu.make_async_remote_copy(
-                src_ref=buffer.at[0], dst_ref=buffer.at[n + 1], send_sem=send_sems.at[n], recv_sem=recv_sems.at[n],
-                device_id=device(o), device_id_type=MESH)
-            copy.start()
-            copies.append(copy)
-        return copies
-
-    def gathered(copies, buffer):
-        for copy in copies:
-            copy.wait_recv()
-        total = buffer[0]
-        for n in range(len(copies)):
-            total = total + buffer[n + 1]
-        return total
-
-    copies = exchange(others, plane_sum, row, plane_send, plane_recv)
-    sent += copies
+            pltpu.make_async_remote_copy(
+                src_ref=buffer.at[0], dst_ref=buffer.at[n + 1], send_sem=send.at[group], recv_sem=recv.at[group],
+                device_id=device(o), device_id_type=MESH).start()
+
+    def gathered(group, buffer):
+        arrived(group)
+        return jnp.sum(buffer[...], axis=0)
+
+    if sizes[0] > 6:
+        pl.semaphore_wait(across, 2)
+    exchange(3, others, plane_sum, row)
 
     for n, u in enumerate((u1, u2)):
         for c in range(3):
@@ -684,12 +688,11 @@
                     for e in range(2):
                         natural[n, c, 2 * e + i, pl.ds(j, 2, stride=2), :] = flat[at8 + 4 * e + 1 : at8 + 4 * e + 3]
 
-    row = gathered(copies, plane_sum)
+    row = gathered(3, plane_sum)
     if rounds:
         pl.semaphore_wait(reached.at[rounds - 1], 2)
-    copies = exchange(along, line_sum, row, line_send, line_recv)
-    sent += copies
-    row = gathered(copies, line_sum)
+    exchange(4, along, line_sum, row)
+    row = gathered(4, line_sum)
     t = solve(row)
     for x in range(4):
         free = wall_in[x] == 0
@@ -701,8 +704,8 @@
     for e in range(2):
         pres_out[e] = v[4 * e + 1 : 4 * e + 3, 0:64]
 
-    for copy in sent:
-        copy.wait_send()
+    for group, ref in enumerate(in_all):
+        pltpu.make_async_copy(ref, ref, send.at[group]).wait()
 
 
 def local(sizes, state_velocity, objective_gradient, wall_flags, design_levels):
@@ -744,9 +747,13 @@
         vm((plane, 1, 128), F32),
         vm((line, 1, 128), F32),
     ]
-    scratch += [pltpu.SemaphoreType.DMA((4,)), pltpu.SemaphoreType.REGULAR((4,))]
-    for count in (26, 8, plane - 1, line - 1):
-        scratch += [pltpu.SemaphoreType.DMA((count,))] * 2
+    scratch += [
+        pltpu.SemaphoreType.DMA((4,)),
+        pltpu.SemaphoreType.REGULAR((4,)),
+        pltpu.SemaphoreType.REGULAR,
+        pltpu.SemaphoreType.DMA((5,)),
+        pltpu.SemaphoreType.DMA((5,)),
+    ]
     return pl.pallas_call(
         functools.partial(kernel, sizes),
         out_shape=(

time: 60.8 us -> 58.7 us (0.965)
  Pallas kernels: 58 us -> 55.9 us
    pallas_call x1, Pallas kernels: 58 us -> 55.9 us  [local(): pl.pallas_call(functools.partial(kernel, sizes), out_shape=(jax.ShapeDtyp...]
where the time goes in v3:
time: 58.7 us; the launch traced here: 58.5 us
  Pallas kernels  55.9 us (95%)
  local copies, waits for them, and re-layouts  1.93 us (3%)
  between operations  0.65 us (1%)
    pallas_call x1, Pallas kernels, local(): pl.pallas_call(functools.partial(kernel, sizes), out_shape=(jax.ShapeDtyp...  55.9 us
    unnamed x4, local copies, waits for them, and re-layouts  1.93 us

profile of v3, /device:TPU:1, one launch (start us, length us, event | category | flops | bytes accessed | tf_op | source)
XLA Modules:
  0.0 58.5 jit_solution(13165014044788494934)
XLA Ops:
  0.6 55.9 %shard_map.59 = (f32[3,4,4,128]{3,2,1,0:T(4,128)}, f32[2,2,64]{2,1,0:T(2,128)}) custom-call(f32[3,4,4,128]{3,2,1,0:T(4,128)} %state_far.1, f32[3,4,4,128]{3,2,1,0:T(4,128)} %grad_far.1, s32[4,4,128]{2,1,0:T(4,128)} %wall_far.1, s32[2,2,64]{2,1,0:T(2,128)} %level_far.1), custom_call_target="tpu_custom_call" | custom-call | tf_op jit(solution)/shard_map/pallas_call | solution.py:757
  56.5 0.0 copy-start
  56.5 1.3 %copy.8 = f32[3,4,4,128]{3,2,1,0:T(4,128)} copy(f32[3,4,4,128]{3,2,1,0:T(4,128)} %get-tuple-element.4) | data formatting | bytes 49152
  57.9 0.0 copy-done
  57.9 0.6 copy.9
Async XLA Ops:
  56.5 1.4 %copy-start = (f32[2,2,64]{2,1,0:T(2,128)S(1)}, f32[2,2,64]{2,1,0:T(2,128)}, u32[]{:S(2)}) copy-start(f32[2,2,64]{2,1,0:T(2,128)} %get-tuple-element.5) | copy-start | bytes 3076

commit v4 on v3

--- a/solution.py
+++ b/solution.py
@@ -18,6 +18,7 @@
 SHAPE = 0.1
 
 OFFSET = math.sqrt(0.15)
+WIDEN = 9
 SPREAD = 3
 LINES = 9
 GATHER = 3
@@ -387,30 +388,30 @@
         for d in (-2, 2):
             pl.semaphore_signal(across, inc=1, device_id=device((d, 0, 0)), device_id_type=MESH)
 
-    def widen(x, carry):
-        inside = jnp.where(x < xlim, 1.0, 0.0).astype(F32)
+    def widen(first):
+        xs = pl.ds(first, WIDEN)
+        column = first + lax.broadcasted_iota(jnp.int32, (WIDEN, 8, 128), 0)
+        inside = column < xlim
         for h in range(2):
             rows8 = pl.ds(8 * h, 8)
-            below = reach[0, x, rows8]
-            above = reach[1, x, rows8]
+            below = reach[0, xs, rows8]
+            above = reach[1, xs, rows8]
+            ok = inside & node_yz[h]
             for f in range(8 if h == 0 else 6):
-                v = nodes[f, x, rows8]
+                v = nodes[f, xs, rows8]
                 go = 8 * f
-                e = jnp.where(lane < 96, pltpu.roll(above, (64 - go) % 128, 1), pltpu.roll(below, (124 - go) % 128, 1))
+                e = jnp.where(lane < 96, pltpu.roll(above, (64 - go) % 128, 2), pltpu.roll(below, (124 - go) % 128, 2))
                 e = jnp.where(lane < 64, v, e)
                 if f == 6:
-                    stiff[0, x] = e
+                    stiff[0, xs] = e
                     continue
-                ok = node_yz[h]
-                if f == 7:
-                    ok = ok & (sub >= 2) & (sub < 7)
-                even[f, x, rows8] = jnp.where(ok, e * inside, 0.0)
-                o = jnp.where(lane < 96, pltpu.roll(above, (60 - go) % 128, 1), pltpu.roll(below, (120 - go) % 128, 1))
-                o = jnp.where(lane < 64, pltpu.roll(v, 64, 1), o)
-                odd[f, x, rows8] = jnp.where(ok, o * inside, 0.0)
-        return carry
-
-    lax.fori_loop(0, 9, widen, 0)
+                here = ok & ((sub >= 2) & (sub < 7)) if f == 7 else ok
+                even[f, xs, rows8] = jnp.where(here, e, 0.0)
+                o = jnp.where(lane < 96, pltpu.roll(above, (60 - go) % 128, 2), pltpu.roll(below, (120 - go) % 128, 2))
+                o = jnp.where(lane < 64, pltpu.roll(v, 64, 2), o)
+                odd[f, xs, rows8] = jnp.where(here, o, 0.0)
+
+    blocks(9, WIDEN, widen)
 
     def to_elements(source, f, x, j):
         return source[f, x, pl.ds(j, 4, stride=2), :]
@@ -452,13 +453,15 @@
         blocks(9, LINES, one)
         return carry
 
-    lax.fori_loop(0, 2, prepare, 0)
+    for chunk in range(2):
+        prepare(chunk, 0)
 
     def first_step(chunk, carry):
         apply_operator(above_floor, u0, None, chunk, wind, slopes, fields, qpoints, ppoints, out, pout)
         return carry
 
-    lax.fori_loop(0, 2, first_step, 0)
+    for chunk in range(2):
+        first_step(chunk, 0)
 
     low_half = sub < 4
 
@@ -500,7 +503,7 @@
                     u1[0, c, i, j, k] = jnp.where(own_wide, full[i, j] * keep_e[i, j, k], 0.0)
         return carry
 
-    lax.fori_loop(0, 3, finish_first, 0)
+    [finish_first(c, 0) for c in range(3)]
 
     def vertex_mask(i, j):
         ok = own_wide & ((lane < 64) | (lane >= zlim))
@@ -599,7 +602,7 @@
         join_parts(2 * c + 1, odd, c)
         return carry
 
-    lax.fori_loop(0, 3, join_component, 0)
+    [join_component(c, 0) for c in range(3)]
     join_parts(6, even, 3)
     collect(0, u2, narrow)
     for i in range(2):
@@ -613,7 +616,8 @@
         apply_operator(above_floor, u2, p2, chunk, wind, slopes, fields, qpoints, ppoints, out, pout)
         return carry
 
-    lax.fori_loop(0, 2, last_step, 0)
+    for chunk in range(2):
+        last_step(chunk, 0)
 
     def finish_last(c, carry):
         for k in range(2):
@@ -624,7 +628,7 @@
                     u3[0, c, i, j, k] = full[i, j] * keep_e[i, j, k]
         return carry
 
-    lax.fori_loop(0, 3, finish_last, 0)
+    [finish_last(c, 0) for c in range(3)]
     full, _ = close(owners(pout, lambda s, chunk, i, j: s[chunk, i * 2 + j], 1), 1)
     p3[0, 0] = -SCALE * full[0, 0]
 
@@ -706,6 +710,17 @@
 
     for group, ref in enumerate(in_all):
         pltpu.make_async_copy(ref, ref, send.at[group]).wait()
+
+
+def hand_over(vel_in, pres_in, vel_out, pres_out, done):
+    copies = [
+        pltpu.make_async_copy(vel_in, vel_out, done.at[0]),
+        pltpu.make_async_copy(pres_in, pres_out, done.at[1]),
+    ]
+    for copy in copies:
+        copy.start()
+    for copy in copies:
+        copy.wait()
 
 
 def local(sizes, state_velocity, objective_gradient, wall_flags, design_levels):
@@ -754,19 +769,29 @@
         pltpu.SemaphoreType.DMA((5,)),
         pltpu.SemaphoreType.DMA((5,)),
     ]
-    return pl.pallas_call(
+    shapes = (
+        jax.ShapeDtypeStruct((3, 4, 4, 128), F32),
+        jax.ShapeDtypeStruct((2, 2, 64), F32),
+    )
+    grant = 56 * 1024 * 1024
+    iterate = pl.pallas_call(
         functools.partial(kernel, sizes),
-        out_shape=(
-            jax.ShapeDtypeStruct((3, 4, 4, 128), F32),
-            jax.ShapeDtypeStruct((2, 2, 64), F32),
-        ),
+        out_shape=shapes,
         in_specs=[pl.BlockSpec(memory_space=pl.ANY)] * 4,
         out_specs=[pl.BlockSpec(memory_space=pltpu.VMEM)] * 2,
         scratch_shapes=scratch,
         compiler_params=pltpu.CompilerParams(
-            collective_id=0, has_side_effects=True, vmem_limit_bytes=56 * 1024 * 1024
+            collective_id=0, has_side_effects=True, vmem_limit_bytes=grant
         ),
     )(state_velocity, objective_gradient, wall_flags, design_levels)
+    return pl.pallas_call(
+        hand_over,
+        out_shape=shapes,
+        in_specs=[pl.BlockSpec(memory_space=pl.ANY)] * 2,
+        out_specs=[pl.BlockSpec(memory_space=pl.ANY)] * 2,
+        scratch_shapes=[pltpu.SemaphoreType.DMA((2,))],
+        compiler_params=pltpu.CompilerParams(vmem_limit_bytes=grant),
+    )(*iterate)
 
 
 def solution(mesh):

time: 58.7 us -> 57 us (0.971)
  local copies, waits for them, and re-layouts: 1.93 us -> 0 us
    unnamed x4 -> x0, local copies, waits for them, and re-layouts: 1.93 us -> none
    pallas_call x1 -> x2, Pallas kernels: 55.9 us -> 56.1 us  [the longest x1 54.2 us: local(): pl.pallas_call(functools.partial(kernel, sizes), out_shape=shapes, in_spe...]
where the time goes in v4:
time: 57 us; the launch traced here: 56.8 us
  Pallas kernels  56.1 us (98%)
  between operations  0.64 us (1%)
    pallas_call x1, Pallas kernels, local(): pl.pallas_call(functools.partial(kernel, sizes), out_shape=shapes, in_spe...  54.2 us
    pallas_call x1, Pallas kernels, local(): pl.pallas_call(hand_over, out_shape=shapes, in_specs=[pl.BlockSpec(memory...  1.93 us

profile of v4, /device:TPU:1, one launch (start us, length us, event | category | flops | bytes accessed | tf_op | source)
XLA Modules:
  0.0 56.8 jit_solution(15060674021591672591)
XLA Ops:
  0.6 54.2 %shard_map.59 = (f32[3,4,4,128]{3,2,1,0:T(4,128)}, f32[2,2,64]{2,1,0:T(2,128)}) custom-call(f32[3,4,4,128]{3,2,1,0:T(4,128)} %state_far.1, f32[3,4,4,128]{3,2,1,0:T(4,128)} %grad_far.1, s32[4,4,128]{2,1,0:T(4,128)} %wall_far.1, s32[2,2,64]{2,1,0:T(2,128)} %level_far.1), custom_call_target="tpu_custom_call" | custom-call | tf_op jit(solution)/shard_map/pallas_call | solution.py:777
  54.9 1.9 %shard_map.60 = (f32[3,4,4,128]{3,2,1,0:T(4,128)}, f32[2,2,64]{2,1,0:T(2,128)}) custom-call(f32[3,4,4,128]{3,2,1,0:T(4,128)} %get-tuple-element.4.vel_in, f32[2,2,64]{2,1,0:T(2,128)} %get-tuple-element.5.pres_in), custom_call_target="tpu_custom_call" | custom-call | tf_op jit(solution)/shard_map/pallas_call | solution.py:787

commit v5 on v4

--- a/solution.py
+++ b/solution.py
@@ -32,6 +32,8 @@
 
 SOURCE = {-1: (2, 4), 0: (0, 4), 1: (0, 3)}
 TARGET = {-1: (0, 2), 0: (2, 6), 1: (6, 9)}
+
+PART_ROWS = {-1: (4, 0, 3), 0: (2, 2, 5), 1: (2, 6, 1)}
 
 
 def forward_both(a, b, c):
@@ -136,6 +138,8 @@
 
 
 def apply_operator(above_floor, elements, pressures, chunk, state, slopes, fields, qpoints, ppoints, out, pout):
+    low_half = lax.broadcasted_iota(jnp.int32, (8, 128), 0) < 4
+    planes = [0, 1, 2] if chunk == 0 else [0]
     spread(elements, chunk, fields)
     if pressures is not None:
         corner = {}
@@ -177,7 +181,9 @@
             first = back_both(force[c], flux[c][0])
             second = back_value(flux[c][1])
             third = back_value(flux[c][2])
-            for i in range(3):
+            if chunk == 1:
+                first, second, third = [[jnp.where(low_half, v[0], v[2])] for v in (first, second, third)]
+            for i in planes:
                 fields[c, i, 0, lines] = first[i]
                 fields[c, i, 1, lines] = second[i]
                 fields[c, i, 2, lines] = third[i]
@@ -190,25 +196,26 @@
         for q in range(3):
             value.append(
                 back_both(
-                    [fields[at, :, 0, p * 3 + q] for p in range(3)],
-                    [fields[at, :, 1, p * 3 + q] for p in range(3)],
+                    [fields[at, 0 : len(planes), 0, p * 3 + q] for p in range(3)],
+                    [fields[at, 0 : len(planes), 1, p * 3 + q] for p in range(3)],
                 )
             )
-            zslope.append(back_value([fields[at, :, 2, p * 3 + q] for p in range(3)]))
+            zslope.append(back_value([fields[at, 0 : len(planes), 2, p * 3 + q] for p in range(3)]))
         for j in range(3):
             nodes = back_both([value[q][j] for q in range(3)], [zslope[q][j] for q in range(3)])
-            out[chunk, at, :, j, 0] = nodes[0] + last_lane(jnp.where(above_floor, nodes[2], 0.0))
-            out[chunk, at, :, j, 1] = nodes[1]
+            out[chunk, at, 0 : len(planes), j, 0] = nodes[0] + last_lane(jnp.where(above_floor, nodes[2], 0.0))
+            out[chunk, at, 0 : len(planes), j, 1] = nodes[1]
 
     blocks(3, GATHER, gather)
     rows = {}
     for q in range(3):
         sides = []
         for p in range(3):
-            sides.append(back_linear([ppoints[r, p * 3 + q] for r in range(3)]))
-        for i in range(2):
+            v = back_linear([ppoints[r, p * 3 + q] for r in range(3)])
+            sides.append(v if chunk == 0 else [jnp.where(low_half, v[0], v[1])])
+        for i in planes[:2]:
             rows[i, q] = back_linear([sides[p][i] for p in range(3)])
-    for i in range(2):
+    for i in planes[:2]:
         for j in range(2):
             low, high = back_linear([rows[i, q][j] for q in range(3)])
             pout[chunk, i * 2 + j] = low + last_lane(jnp.where(above_floor, high, 0.0))
@@ -262,9 +269,11 @@
     others = [(a, b, 0) for a in range(sizes[0]) for b in range(sizes[1]) if (a, b) != (0, 0)]
     along = [(0, 0, d) for d in range(1, sizes[2])]
     partners = {tuple(d % n for d, n in zip(o, sizes)) for o in NEAR}
-    partners = sorted(partners - {(0, 0, 0)})
-
-    side[...] = jnp.zeros_like(side)
+
+    def far_first(offsets):
+        return sorted(offsets, key=lambda o: (-sum(min(d, n - d) for d, n in zip(o, sizes)), o))
+
+    partners, others, along = far_first(partners - {(0, 0, 0)}), far_first(others), far_first(along)
 
     barrier = pltpu.get_barrier_semaphore()
     for o in partners:
@@ -272,6 +281,12 @@
 
     lane = lax.broadcasted_iota(jnp.int32, (8, 128), 1)
     sub = lax.broadcasted_iota(jnp.int32, (8, 128), 0)
+
+    for n, o in enumerate(PLANE):
+        first, count = PART_ROWS[-o[1]][1:]
+        for lo, hi in ((0, first), (first + count, 8)):
+            if lo < hi:
+                side[n, :, :, lo:hi] = jnp.zeros((7, 5, hi - lo, 128), F32)
 
     for copy in loads:
         copy.wait()
@@ -468,11 +483,13 @@
     def owners(source, at, last):
         total = {}
         for chunk in range(2):
-            for i in range(last + 1):
+            for i in range(last + 1) if chunk == 0 else (0,):
                 v = [at(source, chunk, i, j) for j in range(last + 1)]
                 total[chunk, i, 0] = v[0] + last_row(v[last])
                 for j in range(1, last):
                     total[chunk, i, j] = v[j]
+        for j in range(last):
+            total[1, last, j] = total[1, 0, j]
         return total
 
     def close(total, last):
@@ -560,7 +577,7 @@
     for n, o in enumerate(PLANE):
         sx, sy = -o[0], -o[1]
         xs, xe = {-1: (2, 5), 0: (0, 5), 1: (0, 1)}[sx]
-        ys, ty, count = {-1: (4, 0, 3), 0: (2, 2, 5), 1: (2, 6, 1)}[sy]
+        ys, ty, count = PART_ROWS[sy]
         pltpu.make_async_remote_copy(
             src_ref=block.at[:, xs:xe, ys : ys + count], dst_ref=side.at[n, :, 0 : xe - xs, ty : ty + count],
             send_sem=send.at[2], recv_sem=recv.at[2], device_id=device(o), device_id_type=MESH).start()
@@ -664,15 +681,15 @@
     row = jnp.where(single == 10, total, row)
 
     def exchange(group, offsets, buffer, value):
-        buffer[0] = value
+        buffer[0:1] = value
         for n, o in enumerate(offsets):
             pltpu.make_async_remote_copy(
-                src_ref=buffer.at[0], dst_ref=buffer.at[n + 1], send_sem=send.at[group], recv_sem=recv.at[group],
+                src_ref=buffer.at[0:1], dst_ref=buffer.at[n + 1 : n + 2], send_sem=send.at[group], recv_sem=recv.at[group],
                 device_id=device(o), device_id_type=MESH).start()
 
     def gathered(group, buffer):
         arrived(group)
-        return jnp.sum(buffer[...], axis=0)
+        return jnp.sum(buffer[...], axis=0, keepdims=True)
 
     if sizes[0] > 6:
         pl.semaphore_wait(across, 2)
@@ -712,15 +729,13 @@
         pltpu.make_async_copy(ref, ref, send.at[group]).wait()
 
 
-def hand_over(vel_in, pres_in, vel_out, pres_out, done):
-    copies = [
-        pltpu.make_async_copy(vel_in, vel_out, done.at[0]),
-        pltpu.make_async_copy(pres_in, pres_out, done.at[1]),
-    ]
-    for copy in copies:
-        copy.start()
-    for copy in copies:
-        copy.wait()
+def hand_over(vel_in, pres_in, vel_out, pres_out, vel, pres, done):
+    for stage in (((vel_in, vel), (pres_in, pres)), ((vel, vel_out), (pres, pres_out))):
+        copies = [pltpu.make_async_copy(a, b, done.at[n]) for n, (a, b) in enumerate(stage)]
+        for copy in copies:
+            copy.start()
+        for copy in copies:
+            copy.wait()
 
 
 def local(sizes, state_velocity, objective_gradient, wall_flags, design_levels):
@@ -759,8 +774,8 @@
         vm((7, 5) + tile, F32),
         vm((8, 7, 5) + tile, F32),
         vm((2, 3, 4) + tile, F32),
-        vm((plane, 1, 128), F32),
-        vm((line, 1, 128), F32),
+        vm((plane, 128), F32),
+        vm((line, 128), F32),
     ]
     scratch += [
         pltpu.SemaphoreType.DMA((4,)),
@@ -789,7 +804,7 @@
         out_shape=shapes,
         in_specs=[pl.BlockSpec(memory_space=pl.ANY)] * 2,
         out_specs=[pl.BlockSpec(memory_space=pl.ANY)] * 2,
-        scratch_shapes=[pltpu.SemaphoreType.DMA((2,))],
+        scratch_shapes=[vm((3, 4, 4, 128), F32), vm((2, 2, 64), F32), pltpu.SemaphoreType.DMA((2,))],
         compiler_params=pltpu.CompilerParams(vmem_limit_bytes=grant),
     )(*iterate)
 

time: 57 us -> 56.4 us (0.989)
  Pallas kernels: 56.1 us -> 55.5 us
where the time goes in v5:
time: 56.4 us; the launch traced here: 56.1 us
  Pallas kernels  55.5 us (98%)
  between operations  0.64 us (1%)
    pallas_call x1, Pallas kernels, local(): pl.pallas_call(functools.partial(kernel, sizes), out_shape=shapes, in_spe...  54.1 us
    pallas_call x1, Pallas kernels, local(): pl.pallas_call(hand_over, out_shape=shapes, in_specs=[pl.BlockSpec(memory...  1.37 us

profile of v5, /device:TPU:1, one launch (start us, length us, event | category | flops | bytes accessed | tf_op | source)
XLA Modules:
  0.0 56.1 jit_solution(3059005602753713164)
XLA Ops:
  0.6 54.1 %shard_map.59 = (f32[3,4,4,128]{3,2,1,0:T(4,128)}, f32[2,2,64]{2,1,0:T(2,128)}) custom-call(f32[3,4,4,128]{3,2,1,0:T(4,128)} %state_far.1, f32[3,4,4,128]{3,2,1,0:T(4,128)} %grad_far.1, s32[4,4,128]{2,1,0:T(4,128)} %wall_far.1, s32[2,2,64]{2,1,0:T(2,128)} %level_far.1), custom_call_target="tpu_custom_call" | custom-call | tf_op jit(solution)/shard_map/pallas_call | solution.py:792
  54.7 1.4 %shard_map.60 = (f32[3,4,4,128]{3,2,1,0:T(4,128)}, f32[2,2,64]{2,1,0:T(2,128)}) custom-call(f32[3,4,4,128]{3,2,1,0:T(4,128)} %get-tuple-element.4.vel_in, f32[2,2,64]{2,1,0:T(2,128)} %get-tuple-element.5.pres_in), custom_call_target="tpu_custom_call" | custom-call | tf_op jit(solution)/shard_map/pallas_call | solution.py:802

commit v6 on v5

--- a/solution.py
+++ b/solution.py
@@ -661,7 +661,9 @@
                         sums[n] = sums[n] + v[a] * v[b]
         return tuple(sums)
 
-    sums = list(lax.fori_loop(0, 3, products, tuple(jnp.zeros((8, 128), F32) for _ in pairs)))
+    sums = [jnp.zeros((8, 128), F32) for _ in pairs]
+    for c in range(3):
+        sums = list(products(c, sums))
     ps = [None, p1[0, 0], p2[0, 0], p3[0, 0]]
     for n, (a, b) in enumerate(pairs):
         if a:

time: 56.4 us -> 56.3 us (level)
  no operation moved by 1% of the time
where the time goes in v6:
time: 56.3 us; the launch traced here: 56 us
  Pallas kernels  55.4 us (98%)
  between operations  0.64 us (1%)
    pallas_call x1, Pallas kernels, local(): pl.pallas_call(functools.partial(kernel, sizes), out_shape=shapes, in_spe...  54 us
    pallas_call x1, Pallas kernels, local(): pl.pallas_call(hand_over, out_shape=shapes, in_specs=[pl.BlockSpec(memory...  1.37 us

profile of v6, /device:TPU:1, one launch (start us, length us, event | category | flops | bytes accessed | tf_op | source)
XLA Modules:
  0.0 56.0 jit_solution(8317218739261956432)
XLA Ops:
  0.6 54.0 %shard_map.59 = (f32[3,4,4,128]{3,2,1,0:T(4,128)}, f32[2,2,64]{2,1,0:T(2,128)}) custom-call(f32[3,4,4,128]{3,2,1,0:T(4,128)} %state_far.1, f32[3,4,4,128]{3,2,1,0:T(4,128)} %grad_far.1, s32[4,4,128]{2,1,0:T(4,128)} %wall_far.1, s32[2,2,64]{2,1,0:T(2,128)} %level_far.1), custom_call_target="tpu_custom_call" | custom-call | tf_op jit(solution)/shard_map/pallas_call | solution.py:794
  54.7 1.4 %shard_map.60 = (f32[3,4,4,128]{3,2,1,0:T(4,128)}, f32[2,2,64]{2,1,0:T(2,128)}) custom-call(f32[3,4,4,128]{3,2,1,0:T(4,128)} %get-tuple-element.4.vel_in, f32[2,2,64]{2,1,0:T(2,128)} %get-tuple-element.5.pres_in), custom_call_target="tpu_custom_call" | custom-call | tf_op jit(solution)/shard_map/pallas_call | solution.py:804
